TPU v7x, 32 devices: a whole 2x2x4 slice. The times are simulated.
32 devices in a mesh: parts: 2 (over x), seq: 16 (over z, y, core).
Axes of the slice: x: 2, y: 2, z: 4, core: 2. Of those that a mesh axis runs over, the one named last changes fastest.
Arguments:
- prefix: bfloat16 [64, 128, 4608], P(('parts', 'seq')), parts along dimension 0, may hold values from -6 to 6
- backbone_gain: float32 [4608], replicated, may hold values from 0.5 to 2
- kv_weight: bfloat16 [4608, 2048], P('seq'), may hold values from -8 to 8
- lengths: int32 [64], P('parts'), parts along dimension 0, may hold values from 1 to 128, as said below
- assign: int32 [64], P('parts'), parts along dimension 0, may hold values from 0 to 31, each once
- actions: float32 [64, 2, 50, 32], P(('parts', 'seq')), parts along dimension 0, may hold values from -6 to 6
- flow_noise: float32 [64, 2, 50, 32], P(('parts', 'seq')), parts along dimension 0, may hold values from -6 to 6
- timesteps: float32 [64, 2], P(('parts', 'seq')), parts along dimension 0, may hold values from 0 to 1
- expert_gain: float32 [1024], replicated, may hold values from 0.5 to 2
- action_weight: bfloat16 [32, 1024], replicated, may hold values from -1 to 1
- query_weight: bfloat16 [1024, 2048], replicated, may hold values from -0.1875 to 0.1875
- grad_attended: bfloat16 [64, 2, 50, 2048], P(('parts', 'seq')), parts along dimension 0, may hold values from -6 to 6
Outputs:
- attended: bfloat16 [64, 2, 50, 2048], P(('parts', 'seq')), parts along dimension 0
- grad_prefix: bfloat16 [64, 128, 4608], P(('parts', 'seq')), parts along dimension 0
- grad_query: bfloat16 [64, 2, 50, 2048], P(('parts', 'seq')), parts along dimension 0
There are 2 independent parts, one for each index of `parts`. A program takes and returns all parts, laid end to end along the dimension named above; an argument that names none is the same for every part. Nothing has to cross between parts.
Inputs may be any that keep to these rules, and one draw needn't show every extreme that they name: `lengths`: some episode has length 1 and some has length 128. `assign`: a permutation; expert slot j is held by the device of seq with index j // 2.
All inputs are finite; a program needn't handle non-finite values.
Results may differ from a plain program's by a relative error of at most 0.012.
The roundings to bfloat16 on the way count: a program that leaves them out, or rounds other values in their place, can miss the bound.
Values may be sent and summed in bfloat16 or wider, within the bound.
A program may use at most 128 MiB of HBM per device.

v0:
```python
import math

import jax
import jax.numpy as jnp
from jax import lax
from jax.sharding import PartitionSpec as P

KV_HEADS = 8
HEAD = 128


def time_features(times_in, model_width):
    half_width = model_width // 2
    ladder = jnp.arange(half_width, dtype=jnp.float32)
    frequency = jnp.exp(-math.log(10000.0) * ladder / half_width)
    angles = times_in[:, None] * 1000.0 * frequency[None, :]
    return jnp.concatenate([jnp.sin(angles), jnp.cos(angles)], axis=-1)


def expert_queries(
    actions, flow_noise, times_in, expert_gain, action_weight, query_weight, head_dim
):
    batch_count, samples, horizon, action_dim = actions.shape
    model_width = action_weight.shape[1]
    flat_times = times_in.reshape(batch_count * samples)
    mixing = flat_times[:, None, None]
    noisy_actions = mixing * flow_noise.reshape(batch_count * samples, horizon, action_dim) + (
        1.0 - mixing
    ) * actions.reshape(batch_count * samples, horizon, action_dim)
    embedded = jnp.dot(
        noisy_actions.reshape(-1, action_dim).astype(jnp.bfloat16),
        action_weight,
        preferred_element_type=jnp.float32,
    )
    hidden = (
        embedded.reshape(batch_count * samples, horizon, model_width)
        + time_features(flat_times, model_width)[:, None, :]
    )
    inverse_rms = lax.rsqrt(jnp.mean(hidden * hidden, axis=-1, keepdims=True) + 1e-06)
    normed = (hidden * inverse_rms * expert_gain).astype(jnp.bfloat16).reshape(-1, model_width)
    queries = (
        jnp.dot(normed, query_weight, preferred_element_type=jnp.float32) * head_dim ** (-0.5)
    ).astype(jnp.bfloat16)
    return queries.reshape(batch_count, samples * horizon, query_weight.shape[1])


def attend(queries, keyval, length, upstream, kv_heads):
    batch_count, row_count, q_width = queries.shape
    positions = keyval.shape[1]
    kv_width = keyval.shape[2] // 2
    head_dim = kv_width // kv_heads
    group_size = q_width // kv_width
    score_scale = head_dim ** (-0.5)
    query_heads = queries.reshape(batch_count, row_count, kv_heads, group_size, head_dim)
    key_rows = keyval[:, :, :kv_width].reshape(batch_count, positions, kv_heads, head_dim)
    value_rows = keyval[:, :, kv_width:].reshape(batch_count, positions, kv_heads, head_dim)
    scores = jnp.einsum(
        "bakgd,blkd->bkgal", query_heads, key_rows, preferred_element_type=jnp.float32
    )
    visible = (jnp.arange(positions, dtype=jnp.int32)[None, :] < length[:, None])[
        :, None, None, None, :
    ]
    masked = jnp.where(visible, scores, -1e30)
    row_top = jnp.max(masked, axis=-1, keepdims=True)
    exps = jnp.where(visible, jnp.exp(masked - row_top), 0.0)
    probabilities = exps / jnp.sum(exps, axis=-1, keepdims=True)
    rounded = probabilities.astype(jnp.bfloat16)
    attended = (
        jnp.einsum("bkgal,blkd->bakgd", rounded, value_rows, preferred_element_type=jnp.float32)
        .astype(jnp.bfloat16)
        .reshape(batch_count, row_count, q_width)
    )
    upstream_heads = upstream.reshape(batch_count, row_count, kv_heads, group_size, head_dim)
    grad_prob = jnp.einsum(
        "bakgd,blkd->bkgal", upstream_heads, value_rows, preferred_element_type=jnp.float32
    )
    grad_value = jnp.einsum(
        "bkgal,bakgd->blkd", rounded, upstream_heads, preferred_element_type=jnp.float32
    )
    grad_score = (
        probabilities * (grad_prob - jnp.sum(grad_prob * probabilities, axis=-1, keepdims=True))
    ).astype(jnp.bfloat16)
    grad_query = (
        (
            jnp.einsum(
                "bkgal,blkd->bakgd", grad_score, key_rows, preferred_element_type=jnp.float32
            )
            * score_scale
        )
        .astype(jnp.bfloat16)
        .reshape(batch_count, row_count, q_width)
    )
    grad_key = jnp.einsum(
        "bkgal,bakgd->blkd", grad_score, query_heads, preferred_element_type=jnp.float32
    )
    grad_kv = jnp.concatenate(
        [
            grad_key.reshape(batch_count, positions, kv_width),
            grad_value.reshape(batch_count, positions, kv_width),
        ],
        axis=-1,
    ).astype(jnp.bfloat16)
    return (attended, grad_kv, grad_query)


def route_keys(block, ordering):
    spread = lax.all_to_all(block, "seq", split_axis=2, concat_axis=0, tiled=True)
    arranged = jnp.take(spread, ordering, axis=0)
    return lax.all_to_all(arranged, "seq", split_axis=0, concat_axis=2, tiled=True)


def shards(
    prefix,
    backbone_gain,
    kv_weight,
    lengths,
    assign,
    actions,
    flow_noise,
    timesteps,
    expert_gain,
    action_weight,
    query_weight,
    grad_attended,
):
    position = lax.axis_index("seq")
    owned_count, positions, model_width = prefix.shape
    episodes = assign.shape[0]
    doubled = kv_weight.shape[1]
    samples, horizon, q_width = (
        grad_attended.shape[1],
        grad_attended.shape[2],
        grad_attended.shape[3],
    )
    prefix_f32 = prefix.astype(jnp.float32)
    inverse_rms = lax.rsqrt(jnp.mean(prefix_f32 * prefix_f32, axis=-1, keepdims=True) + 1e-06)
    normed = (
        (prefix_f32 * inverse_rms * backbone_gain)
        .astype(jnp.bfloat16)
        .reshape(owned_count * positions, model_width)
    )
    whole_weight = lax.all_gather(kv_weight, "seq", axis=0, tiled=True)
    product = jnp.dot(normed, whole_weight, preferred_element_type=jnp.float32)
    keyval = product.astype(jnp.bfloat16).reshape(owned_count, positions, doubled)
    queries = expert_queries(
        actions, flow_noise, timesteps, expert_gain, action_weight, query_weight, HEAD
    )
    upstream = grad_attended.reshape(owned_count, samples * horizon, q_width)
    slot_index = jnp.arange(episodes, dtype=jnp.int32)
    matches = assign[None, :] == slot_index[:, None]
    inverse = jnp.sum(jnp.where(matches, slot_index[None, :], 0), axis=1)
    my_slots = lax.dynamic_slice_in_dim(assign, position * owned_count, owned_count)
    chosen = slot_index[None, :] == my_slots[:, None]
    owned_len = jnp.sum(jnp.where(chosen, lengths[None, :], 0), axis=1)
    owned_kv = route_keys(keyval, assign)
    attended, grad_kv, grad_query = attend(queries, owned_kv, owned_len, upstream, KV_HEADS)
    grad_keyval = route_keys(grad_kv, inverse)
    restored = grad_keyval.reshape(owned_count * positions, doubled)
    grad_normed = lax.dot_general(
        restored, whole_weight, (((1,), (1,)), ((), ())), preferred_element_type=jnp.float32
    )
    gated = grad_normed.reshape(owned_count, positions, model_width) * backbone_gain
    grad_prefix = (
        inverse_rms * gated
        - prefix_f32 * inverse_rms**3 * jnp.mean(prefix_f32 * gated, axis=-1, keepdims=True)
    ).astype(jnp.bfloat16)
    shape_out = (owned_count, samples, horizon, q_width)
    return (attended.reshape(shape_out), grad_prefix, grad_query.reshape(shape_out))


def solution(mesh):
    placed = (
        P(("parts", "seq"), None, None),
        P(),
        P("seq", None),
        P("parts"),
        P("parts"),
        P(("parts", "seq"), None, None, None),
        P(("parts", "seq"), None, None, None),
        P(("parts", "seq"), None),
        P(),
        P(),
        P(),
        P(("parts", "seq"), None, None, None),
    )
    return jax.shard_map(
        shards,
        mesh=mesh,
        in_specs=placed,
        out_specs=(
            P(("parts", "seq"), None, None, None),
            P(("parts", "seq"), None, None),
            P(("parts", "seq"), None, None, None),
        ),
        check_vma=False,
    )
```

profile of v0, /device:TPU:21, one launch (start us, length us, event | category | flops | bytes accessed | tf_op | source)
XLA Modules:
  0.0 299.3 jit_solution(9540587795098782000)
XLA Ops:
  7.2 0.7 all-gather.2.cloned.1.call-update
  7.9 2.2 fusion.6
  10.2 2.0 fusion.8
  12.2 97.7 %all-gather.2.cloned.1.call-done = bf16[4608,2048]{1,0:T(8,128)(2,1)} async-done(((bf16[288,2048]{1,0:T(8,128)(2,1)}), bf16[4608,2048]{1,0:T(8,128)(2,1)}) %all-gather.2.cloned.1.call-update) | async-done | bytes 18874384 | tf_op jit(solution)/shard_map/all_gather | solution.py:142
  109.9 9.7 %convolution_convert_fusion = bf16[256,2048]{1,0:T(8,128)(2,1)S(1)} fusion(bf16[256,4608]{1,0:T(8,128)(2,1)} %bitcast.117, bf16[4608,2048]{1,0:T(8,128)(2,1)} %all-gather.2.cloned.1.call-done), kind=kOutput, calls=%fused_computation.18 | convolution fusion | flops 4832362496 | bytes 22282240 | tf_op jit(solution)/shard_map/dot_general | solution.py:143
  119.5 2.0 copy.72
  121.5 5.3 %all-to-all-start = ((bf16[2,128,2048]{1,0,2:T(2,128)(2,1)}), bf16[2,128,2048]{1,0,2:T(2,128)(2,1)S(1)}, u32[]{:S(2)}, u32[]{:S(2)}) async-start(bf16[2,128,2048]{1,0,2:T(2,128)(2,1)} %copy.72), calls=%async_computation | async-start | bytes 2097152 | tf_op jit(solution)/shard_map/all_to_all | solution.py:107
  127.0 2.9 copy.80
  129.9 3.8 %reshape_reshape.14 = bf16[2,100,8,2,128]{4,3,2,0,1:T(2,128)(2,1)} reshape(bf16[2,2,50,2048]{3,0,2,1:T(2,128)(2,1)} %copy.80) | data formatting | bytes 1638400 | tf_op jit(solution)/shard_map/reshape;reshape | solution.py:73
  133.7 0.6 dynamic_slice.3
  135.3 14.4 %all-to-all-done = bf16[2,128,2048]{1,0,2:T(2,128)(2,1)S(1)} async-done(((bf16[2,128,2048]{1,0,2:T(2,128)(2,1)}), bf16[2,128,2048]{1,0,2:T(2,128)(2,1)S(1)}, u32[]{:S(2)}, u32[]{:S(2)}) %all-to-all-start) | async-done | bytes 1048608 | tf_op jit(solution)/shard_map/all_to_all | solution.py:107
  149.8 1.1 copy.73
  150.9 2.3 copy.74
  153.2 2.0 gather_fusion
  155.2 1.8 broadcast_select_fusion.1
  157.0 6.9 %all-to-all-start.1 = ((bf16[32,128,128]{2,1,0:T(8,128)(2,1)}), bf16[32,128,128]{2,1,0:T(8,128)(2,1)S(1)}, u32[]{:S(2)}, u32[]{:S(2)}) async-start(bf16[32,128,128]{2,1,0:T(8,128)(2,1)} %broadcast_select_fusion.1), calls=%async_computation.1 | async-start | bytes 2097152 | tf_op jit(solution)/shard_map/all_to_all | solution.py:109
  163.9 0.8 multiply_sine_fusion
  164.7 0.9 fusion.40
  166.1 0.9 multiply_convert_fusion.1
  167.0 1.9 reshape.142
  168.9 4.3 %fusion.13 = bf16[200,2048]{1,0:T(8,128)(2,1)} fusion(bf16[200,1024]{1,0:T(8,128)(2,1)} %reshape.142, bf16[1024,2048]{1,0:T(8,128)(2,1)} %param.24), kind=kOutput, calls=%fused_computation.19 | convolution fusion | flops 839680000 | bytes 5423104 | tf_op jit(solution)/shard_map/dot_general | solution.py:42
  173.1 3.3 %reshape_reshape.12 = bf16[2,100,8,2,128]{4,3,2,1,0:T(2,128)(2,1)} reshape(bf16[200,2048]{1,0:T(8,128)(2,1)} %fusion.13) | data formatting | bytes 1638400 | tf_op jit(solution)/shard_map/reshape;reshape | solution.py:54
  176.7 10.1 %all-to-all-done.1 = bf16[32,128,128]{2,1,0:T(8,128)(2,1)S(1)} async-done(((bf16[32,128,128]{2,1,0:T(8,128)(2,1)}), bf16[32,128,128]{2,1,0:T(8,128)(2,1)S(1)}, u32[]{:S(2)}, u32[]{:S(2)}) %all-to-all-start.1) | async-done | bytes 1048608 | tf_op jit(solution)/shard_map/all_to_all | solution.py:109
  186.8 1.3 copy.75
  188.1 1.3 fusion.49
  189.4 3.4 %fusion.50 = (f32[2,8,2,100]{3,2,1,0:T(2,128)S(1)}, f32[2,8,2,100,128]{4,3,2,1,0:T(8,128)}) fusion(pred[2,128]{1,0:T(4,128)(4,1)S(1)} %iota_compare_fusion.1, bf16[2,128,8,128,1]{1,3,4,2,0:T(8,128)(2,1)S(1)} %bitcast.119, bf16[2,100,8,2,128]{4,3,2,1,0:T(2,128)(2,1)} %reshape_reshape.12), kind=kOutput, calls=%fused_computation.85 | convolution fusion | flops 106496128 | bytes 2994944 | tf_op jit(solution)/shard_map/sub | solution.py:65
  192.8 2.8 fusion.25
  196.3 1.3 fusion.15
  197.6 1.1 fusion.17
  199.8 10.3 %pad_maximum_fusion = bf16[2,128,2048]{1,0,2:T(2,128)(2,1)} fusion(bf16[2,128,1024]{1,0,2:T(2,128)(2,1)S(1)} %copy.86, bf16[2,128,1024]{1,0,2:T(2,128)(2,1)S(1)} %copy.85), kind=kLoop, calls=%fused_computation.41 | loop fusion | flops 524288 | bytes 2097152 | tf_op jit(solution)/shard_map/concatenate | solution.py:96
  210.1 6.9 %all-to-all-start.2 = ((bf16[2,128,2048]{1,0,2:T(2,128)(2,1)}), bf16[2,128,2048]{1,0,2:T(2,128)(2,1)}, u32[]{:S(2)}, u32[]{:S(2)}) async-start(bf16[2,128,2048]{1,0,2:T(2,128)(2,1)} %pad_maximum_fusion), calls=%async_computation.2 | async-start | bytes 2097152 | tf_op jit(solution)/shard_map/all_to_all | solution.py:107
  217.2 22.7 %all-to-all-done.2 = bf16[2,128,2048]{1,0,2:T(2,128)(2,1)} async-done(((bf16[2,128,2048]{1,0,2:T(2,128)(2,1)}), bf16[2,128,2048]{1,0,2:T(2,128)(2,1)}, u32[]{:S(2)}, u32[]{:S(2)}) %all-to-all-start.2) | async-done | bytes 1048608 | tf_op jit(solution)/shard_map/all_to_all | solution.py:107
  239.9 2.4 copy.87
  242.3 2.3 copy.88
  244.6 2.9 gather_fusion.1
  247.5 2.4 broadcast_select_fusion
  249.9 7.0 %all-to-all-start.3 = ((bf16[32,128,128]{2,1,0:T(8,128)(2,1)}), bf16[32,128,128]{2,1,0:T(8,128)(2,1)}, u32[]{:S(2)}, u32[]{:S(2)}) async-start(bf16[32,128,128]{2,1,0:T(8,128)(2,1)} %broadcast_select_fusion), calls=%async_computation.3 | async-start | bytes 2097152 | tf_op jit(solution)/shard_map/all_to_all | solution.py:109
  256.9 2.3 fusion.22
  259.2 1.5 copy.79
  260.7 3.7 %reshape_reshape.13 = bf16[2,2,50,2048]{3,0,2,1:T(2,128)(2,1)} reshape(bf16[2,100,8,2,128]{4,3,2,0,1:T(2,128)(2,1)} %copy.79) | data formatting | bytes 1638400 | tf_op jit(solution)/shard_map/reshape;reshape | solution.py:168
  264.4 2.9 copy.92
  267.3 1.6 fusion.23
  268.9 0.6 copy.91
  269.6 1.1 reshape_reshape.15
  270.7 2.9 copy.93
  273.5 6.2 %all-to-all-done.3 = bf16[32,128,128]{2,1,0:T(8,128)(2,1)} async-done(((bf16[32,128,128]{2,1,0:T(8,128)(2,1)}), bf16[32,128,128]{2,1,0:T(8,128)(2,1)}, u32[]{:S(2)}, u32[]{:S(2)}) %all-to-all-start.3) | async-done | bytes 1048608 | tf_op jit(solution)/shard_map/all_to_all | solution.py:109
  279.8 9.6 %fusion.12 = (f32[2,128]{1,0:T(2,128)S(1)}, f32[2,128,4608]{2,1,0:T(8,128)S(1)}) fusion(bf16[2,128,4608]{2,1,0:T(8,128)(2,1)S(1)} %copy-done.2, f32[4608]{0:T(1024)S(1)} %copy-done.10, bf16[4608,2048]{1,0:T(8,128)(2,1)} %all-gather.2.cloned.1.call-done, bf16[16,2,16,8,128]{4,3,2,1,0:T(8,128)(2,1)} %bitcast.47), kind=kOutput, calls=%fused_computation.16 | convolution fusion | flops 4836556800 | bytes 27020288 | tf_op jit(solution)/shard_map/dot_general | solution.py:159
  289.4 3.0 %fusion.11 = bf16[2,128,4608]{2,1,0:T(8,128)(2,1)} fusion(bf16[2,128,4608]{2,1,0:T(8,128)(2,1)S(1)} %copy-done.2, f32[2,128,4608]{2,1,0:T(8,128)S(1)} %get-tuple-element.31, f32[2,128]{1,0:T(2,128)S(1)} %broadcast_multiply_fusion, f32[2,128]{1,0:T(2,128)S(1)} %get-tuple-element.20, f32[2,128]{1,0:T(2,128)S(1)} %get-tuple-element.21), kind=kLoop, calls=%fused_computation.15 | loop fusion | flops 7077888 | bytes 9440256 | tf_op jit(solution)/shard_map/convert_element_type | solution.py:166
  (57 shorter events, 3.7 us)
Async XLA Ops:
  7.2 158.5 %copy-start = (bf16[32,1024]{1,0:T(8,128)(2,1)S(1)}, bf16[32,1024]{1,0:T(8,128)(2,1)}, u32[]{:S(2)}) copy-start(bf16[32,1024]{1,0:T(8,128)(2,1)} %param.23) | copy-start | bytes 196612
  7.2 3.0 copy-start.2
  7.2 3.0 copy-start.9
  7.2 102.7 %all-gather.2.cloned.1.call-start = ((), (), s32[]{:S(2)}) async-start(), calls=%async_computation.4 | async-start | bytes 20054016 | tf_op jit(solution)/shard_map/all_gather | solution.py:142
  119.5 7.4 %copy-start.13 = (f32[2,2]{1,0:T(2,128)S(1)}, f32[2,2]{1,0:T(2,128)}, u32[]{:S(2)}) copy-start(f32[2,2]{1,0:T(2,128)} %param.21) | copy-start | bytes 52
  121.5 12.1 %copy-start.15 = (s32[32]{0:T(128)S(1)}, s32[32]{0:T(128)}, u32[]{:S(2)}) copy-start(s32[32]{0:T(128)} %param.18) | copy-start | bytes 388
  121.5 28.2 %all-to-all-start = ((bf16[2,128,2048]{1,0,2:T(2,128)(2,1)}), bf16[2,128,2048]{1,0,2:T(2,128)(2,1)S(1)}, u32[]{:S(2)}, u32[]{:S(2)}) async-start(bf16[2,128,2048]{1,0,2:T(2,128)(2,1)} %copy.72), calls=%async_computation | async-start | bytes 2097152 | tf_op jit(solution)/shard_map/all_to_all | solution.py:107
  127.0 23.9 %copy-start.12 = (f32[4]{0:T(128)}, f32[4]{0:T(128)S(1)}, u32[]{:S(2)}) copy-start(f32[4]{0:T(128)S(1)} %mul.143) | copy-start | bytes 52
  155.1 9.6 %copy-start.8 = (f32[2,2,50,32]{2,3,1,0:T(8,128)S(1)}, f32[2,2,50,32]{2,3,1,0:T(8,128)}, u32[]{:S(2)}) copy-start(f32[2,2,50,32]{2,3,1,0:T(8,128)} %param.19) | copy-start | bytes 76804
  155.1 10.9 %copy-start.11 = (f32[1024]{0:T(1024)S(1)}, f32[1024]{0:T(1024)}, u32[]{:S(2)}) copy-start(f32[1024]{0:T(1024)} %param.22) | copy-start | bytes 12292
  157.0 29.8 %all-to-all-start.1 = ((bf16[32,128,128]{2,1,0:T(8,128)(2,1)}), bf16[32,128,128]{2,1,0:T(8,128)(2,1)S(1)}, u32[]{:S(2)}, u32[]{:S(2)}) async-start(bf16[32,128,128]{2,1,0:T(8,128)(2,1)} %broadcast_select_fusion.1), calls=%async_computation.1 | async-start | bytes 2097152 | tf_op jit(solution)/shard_map/all_to_all | solution.py:109
  168.9 7.6 %copy-start.14 = (s32[32]{0:T(128)S(1)}, s32[32]{0:T(128)}, u32[]{:S(2)}) copy-start(s32[32]{0:T(128)} %param.17) | copy-start | bytes 388
  168.9 7.6 %copy-start.17 = (s32[2]{0:T(128)S(1)}, s32[2]{0:T(128)}, u32[]{:S(2)}) copy-start(s32[2]{0:T(128)} %dynamic_slice.3) | copy-start | bytes 28
  189.4 6.3 %copy-start.4 = (bf16[2,128,1024]{1,2,0:T(8,128)(2,1)}, bf16[2,128,1024]{1,2,0:T(8,128)(2,1)S(1)}, u32[]{:S(2)}) copy-start(bf16[2,128,1024]{1,2,0:T(8,128)(2,1)S(1)} %get-tuple-element.16) | copy-start | bytes 1572868
  189.4 6.9 %copy-start.7 = (bf16[2,128,1024]{1,2,0:T(8,128)(2,1)}, bf16[2,128,1024]{1,2,0:T(8,128)(2,1)S(1)}, u32[]{:S(2)}) copy-start(bf16[2,128,1024]{1,2,0:T(8,128)(2,1)S(1)} %get-tuple-element.17) | copy-start | bytes 1572868
  192.8 3.4 %copy-start.5 = (f32[2,8,2,100,128]{4,3,2,1,0:T(8,128)S(1)}, f32[2,8,2,100,128]{4,3,2,1,0:T(8,128)}, u32[]{:S(2)}) copy-start(f32[2,8,2,100,128]{4,3,2,1,0:T(8,128)} %get-tuple-element.27) | copy-start | bytes 4915204
  192.8 3.4 %copy-start.6 = (bf16[2,100,8,2,128]{4,3,2,0,1:T(2,128)(2,1)S(1)}, bf16[2,100,8,2,128]{4,3,2,0,1:T(2,128)(2,1)}, u32[]{:S(2)}) copy-start(bf16[2,100,8,2,128]{4,3,2,0,1:T(2,128)(2,1)} %reshape_reshape.14) | copy-start | bytes 2457604
  197.6 1.1 copy-start.3
  199.8 17.3 %copy-start.16 = (s32[32]{0:T(128)S(1)}, s32[32]{0:T(128)}, u32[]{:S(2)}) copy-start(s32[32]{0:T(128)} %param.18) | copy-start | bytes 388
  210.1 29.8 %all-to-all-start.2 = ((bf16[2,128,2048]{1,0,2:T(2,128)(2,1)}), bf16[2,128,2048]{1,0,2:T(2,128)(2,1)}, u32[]{:S(2)}, u32[]{:S(2)}) async-start(bf16[2,128,2048]{1,0,2:T(2,128)(2,1)} %pad_maximum_fusion), calls=%async_computation.2 | async-start | bytes 2097152 | tf_op jit(solution)/shard_map/all_to_all | solution.py:107
  249.9 29.9 %all-to-all-start.3 = ((bf16[32,128,128]{2,1,0:T(8,128)(2,1)}), bf16[32,128,128]{2,1,0:T(8,128)(2,1)}, u32[]{:S(2)}, u32[]{:S(2)}) async-start(bf16[32,128,128]{2,1,0:T(8,128)(2,1)} %broadcast_select_fusion), calls=%async_computation.3 | async-start | bytes 2097152 | tf_op jit(solution)/shard_map/all_to_all | solution.py:109
  268.9 10.8 %copy-start.10 = (f32[4608]{0:T(1024)S(1)}, f32[4608]{0:T(1024)}, u32[]{:S(2)}) copy-start(f32[4608]{0:T(1024)} %param.15) | copy-start | bytes 55300
  289.4 3.0 %copy-start.1 = (bf16[32,1024]{1,0:T(8,128)(2,1)S(1)}, bf16[32,1024]{1,0:T(8,128)(2,1)}, u32[]{:S(2)}) copy-start(bf16[32,1024]{1,0:T(8,128)(2,1)} %param.23) | copy-start | bytes 196612
Sparse Core Ops, SparseCore 0:
  9.6 100.1 all-gather.1
where the time goes:
time: 303 us; the launch traced here: 299 us
  waiting for transfers between devices  152 us (50%)
  local copies, waits for them, and re-layouts  44 us (15%)
  matrix products  35.9 us (12%)
  other arithmetic  27 us (9%)
  starting transfers between devices  26.3 us (9%)
  between operations  14.4 us (5%)
    all_gather x1, waiting for transfers between devices, shards(): whole_weight = lax.all_gather(kv_weight, 'seq', axis=0, tiled=True)  97.7 us
    all_to_all x2, waiting for transfers between devices, route_keys(): lax.all_to_all(block, 'seq', split_axis=2, concat_axis=0, tiled=True)  37.2 us
    all_to_all x2, waiting for transfers between devices, route_keys(): lax.all_to_all(arranged, 'seq', split_axis=0, concat_axis=2, tiled=True)  16.3 us
    all_to_all x2, starting transfers between devices, route_keys(): lax.all_to_all(arranged, 'seq', split_axis=0, concat_axis=2, tiled=True)  14 us
    all_to_all x2, starting transfers between devices, route_keys(): lax.all_to_all(block, 'seq', split_axis=2, concat_axis=0, tiled=True)  12.3 us
    concatenate x1, other arithmetic, attend(): jnp.concatenate([grad_key.reshape(batch_count, positions, kv_width), grad...  10.3 us
    dot_general x1, matrix products, shards(): product = jnp.dot(normed, whole_weight, preferred_element_type=jnp.float32)  9.66 us
    dot_general x1, matrix products, shards(): lax.dot_general(restored, whole_weight, (((1,), (1,)), ((), ())), preferr...  9.58 us
  transfers between devices with their start and end apart: 5, of which 5 were waited for; matrix products, arithmetic and copies ran while one was open for 14% of the time, Pallas kernels for 0%

commit v1 on v0

--- a/solution.py
+++ b/solution.py
@@ -17,18 +17,12 @@
     return jnp.concatenate([jnp.sin(angles), jnp.cos(angles)], axis=-1)
 
 
-def expert_queries(
-    actions, flow_noise, times_in, expert_gain, action_weight, query_weight, head_dim
-):
-    batch_count, samples, horizon, action_dim = actions.shape
+def expert_queries(mixed, times_in, expert_gain, action_weight, query_weight, head_dim):
+    batch_count, samples, horizon, action_dim = mixed.shape
     model_width = action_weight.shape[1]
     flat_times = times_in.reshape(batch_count * samples)
-    mixing = flat_times[:, None, None]
-    noisy_actions = mixing * flow_noise.reshape(batch_count * samples, horizon, action_dim) + (
-        1.0 - mixing
-    ) * actions.reshape(batch_count * samples, horizon, action_dim)
     embedded = jnp.dot(
-        noisy_actions.reshape(-1, action_dim).astype(jnp.bfloat16),
+        mixed.reshape(-1, action_dim).astype(jnp.bfloat16),
         action_weight,
         preferred_element_type=jnp.float32,
     )
@@ -132,6 +126,28 @@
         grad_attended.shape[2],
         grad_attended.shape[3],
     )
+    slot_index = jnp.arange(episodes, dtype=jnp.int32)
+    matches = assign[None, :] == slot_index[:, None]
+    inverse = jnp.sum(jnp.where(matches, slot_index[None, :], 0), axis=1)
+    my_slots = lax.dynamic_slice_in_dim(inverse, position * owned_count, owned_count)
+    owned_len = lax.dynamic_slice_in_dim(lengths, position * owned_count, owned_count)
+
+    mixing = timesteps[:, :, None, None]
+    mixed = mixing * flow_noise + (1.0 - mixing) * actions
+    packed = jnp.concatenate(
+        [mixed.reshape(owned_count, -1), timesteps], axis=1
+    )
+    gathered = lax.all_gather(packed, "seq", axis=0, tiled=True)
+    own_packed = jnp.take(gathered, my_slots, axis=0)
+    whole_weight = lax.all_gather(kv_weight, "seq", axis=0, tiled=True)
+    upstream = route_keys(
+        grad_attended.reshape(owned_count, samples * horizon, q_width), inverse
+    )
+    own_mixed = own_packed[:, :-samples].reshape(owned_count, samples, horizon, -1)
+    queries = expert_queries(
+        own_mixed, own_packed[:, -samples:], expert_gain, action_weight, query_weight, HEAD
+    )
+
     prefix_f32 = prefix.astype(jnp.float32)
     inverse_rms = lax.rsqrt(jnp.mean(prefix_f32 * prefix_f32, axis=-1, keepdims=True) + 1e-06)
     normed = (
@@ -139,23 +155,12 @@
         .astype(jnp.bfloat16)
         .reshape(owned_count * positions, model_width)
     )
-    whole_weight = lax.all_gather(kv_weight, "seq", axis=0, tiled=True)
     product = jnp.dot(normed, whole_weight, preferred_element_type=jnp.float32)
     keyval = product.astype(jnp.bfloat16).reshape(owned_count, positions, doubled)
-    queries = expert_queries(
-        actions, flow_noise, timesteps, expert_gain, action_weight, query_weight, HEAD
-    )
-    upstream = grad_attended.reshape(owned_count, samples * horizon, q_width)
-    slot_index = jnp.arange(episodes, dtype=jnp.int32)
-    matches = assign[None, :] == slot_index[:, None]
-    inverse = jnp.sum(jnp.where(matches, slot_index[None, :], 0), axis=1)
-    my_slots = lax.dynamic_slice_in_dim(assign, position * owned_count, owned_count)
-    chosen = slot_index[None, :] == my_slots[:, None]
-    owned_len = jnp.sum(jnp.where(chosen, lengths[None, :], 0), axis=1)
-    owned_kv = route_keys(keyval, assign)
-    attended, grad_kv, grad_query = attend(queries, owned_kv, owned_len, upstream, KV_HEADS)
-    grad_keyval = route_keys(grad_kv, inverse)
-    restored = grad_keyval.reshape(owned_count * positions, doubled)
+    attended, grad_kv, grad_query = attend(queries, keyval, owned_len, upstream, KV_HEADS)
+    attended = route_keys(attended, assign)
+    grad_query = route_keys(grad_query, assign)
+    restored = grad_kv.reshape(owned_count * positions, doubled)
     grad_normed = lax.dot_general(
         restored, whole_weight, (((1,), (1,)), ((), ())), preferred_element_type=jnp.float32
     )

time: 303 us -> 315 us (1.040)
  waiting for transfers between devices: 152 us -> 88.4 us
  blocking collectives: 0 us -> 49.9 us
  local copies, waits for them, and re-layouts: 44 us -> 60.3 us
  starting transfers between devices: 26.3 us -> 41.8 us
  other arithmetic: 27 us -> 14 us
  matrix products: 35.9 us -> 42 us
    all_gather x1, waiting for transfers between devices: 97.7 us -> 18.3 us  [shards(): whole_weight = lax.all_gather(kv_weight, 'seq', axis=0, tiled=True)]
    all_gather x0 -> x1, blocking collectives: none -> 49.9 us  [shards(): gathered = lax.all_gather(packed, 'seq', axis=0, tiled=True)]
    all_to_all x2 -> x3, waiting for transfers between devices: 16.3 us -> 44.3 us  [route_keys(): lax.all_to_all(arranged, 'seq', split_axis=0, concat_axis=2, tiled=True)]
    all_to_all x2 -> x3, waiting for transfers between devices: 37.2 us -> 25.2 us  [route_keys(): lax.all_to_all(block, 'seq', split_axis=2, concat_axis=0, tiled=True)]
    concatenate x1 -> x0, other arithmetic: 10.3 us -> none  [attend(): jnp.concatenate([grad_key.reshape(batch_count, positions, kv_width), grad...]
    all_to_all x2 -> x3, starting transfers between devices: 14 us -> 23.1 us  [route_keys(): lax.all_to_all(arranged, 'seq', split_axis=0, concat_axis=2, tiled=True)]
    another operation x3 -> x0, local copies, waits for them, and re-layouts: 8.55 us -> none  [the longest x1 3.79 us: attend(): upstream.reshape(batch_count, row_count, kv_heads, group_size, head_dim)]
    reshape x3 -> x6, local copies, waits for them, and re-layouts: 3.08 us -> 10.8 us  [the longest x1 3.66 us: attend(): attended = jnp.einsum('bkgal,blkd->bakgd', rounded, value_rows, preferred...]
  transfers between devices with their start and end apart: 5 -> 7, of which waited for: 5 -> 6; matrix products, arithmetic and copies ran while one was open for 14% -> 23% of each run, Pallas kernels for 0% -> 0%
where the time goes in v1:
time: 315 us; the launch traced here: 311 us
  waiting for transfers between devices  88.4 us (28%)
  local copies, waits for them, and re-layouts  60.3 us (19%)
  blocking collectives  49.9 us (16%)
  matrix products  42 us (13%)
  starting transfers between devices  41.8 us (13%)
  between operations  14.4 us (5%)
  other arithmetic  14 us (4%)
    all_gather x1, blocking collectives, shards(): gathered = lax.all_gather(packed, 'seq', axis=0, tiled=True)  49.9 us
    all_to_all x3, waiting for transfers between devices, route_keys(): lax.all_to_all(arranged, 'seq', split_axis=0, concat_axis=2, tiled=True)  44.3 us
    all_to_all x3, waiting for transfers between devices, route_keys(): lax.all_to_all(block, 'seq', split_axis=2, concat_axis=0, tiled=True)  25.2 us
    all_to_all x3, starting transfers between devices, route_keys(): lax.all_to_all(arranged, 'seq', split_axis=0, concat_axis=2, tiled=True)  23.1 us
    all_to_all x3, starting transfers between devices, route_keys(): lax.all_to_all(block, 'seq', split_axis=2, concat_axis=0, tiled=True)  18.6 us
    all_gather x1, waiting for transfers between devices, shards(): whole_weight = lax.all_gather(kv_weight, 'seq', axis=0, tiled=True)  18.3 us
    all_to_all x9, local copies, waits for them, and re-layouts, route_keys(): lax.all_to_all(block, 'seq', split_axis=2, concat_axis=0, tiled=True)  14.8 us
    unnamed x38, local copies, waits for them, and re-layouts  12.7 us
  transfers between devices with their start and end apart: 7, of which 6 were waited for; matrix products, arithmetic and copies ran while one was open for 23% of the time, Pallas kernels for 0%

profile of v1, /device:TPU:21, one launch (start us, length us, event | category | flops | bytes accessed | tf_op | source)
XLA Modules:
  0.0 310.8 jit_solution(13053232620151400750)
XLA Ops:
  7.9 2.0 copy.150
  9.9 3.0 copy.151
  13.0 6.6 %all-to-all-start.2 = ((bf16[2,100,2048]{1,0,2:T(2,128)(2,1)}), bf16[2,100,2048]{1,0,2:T(2,128)(2,1)S(1)}, u32[]{:S(2)}, u32[]{:S(2)}) async-start(bf16[2,100,2048]{1,0,2:T(2,128)(2,1)} %copy.151), calls=%async_computation.2 | async-start | bytes 2097152 | tf_op jit(solution)/shard_map/all_to_all | solution.py:101
  19.9 49.9 %all-gather = f32[16,2,3202]{2,1,0:T(2,128)} all-gather(f32[1,2,3202]{2,1,0:T(2,128)S(1)} %maximum_bitcast_fusion), channel_id=1, replica_groups=mesh['parts'=2,'seq'=16] {'seq'}, dimensions={0}, use_global_device_ids=true | all-gather | bytes 435472 | tf_op jit(solution)/shard_map/all_gather | solution.py:140
  69.9 2.2 reshape.190
  72.7 1.6 gather_fusion
  76.8 1.9 reshape.146
  79.7 4.1 %fusion.13 = bf16[200,2048]{1,0:T(8,128)(2,1)} fusion(bf16[200,1024]{1,0:T(8,128)(2,1)S(1)} %copy-done.6, bf16[1024,2048]{1,0:T(8,128)(2,1)} %param.24), kind=kOutput, calls=%fused_computation.21 | convolution fusion | flops 839680000 | bytes 5423104 | tf_op jit(solution)/shard_map/dot_general | solution.py:36
  83.8 1.5 copy.185
  85.3 2.4 copy.153
  88.9 1.9 gather_fusion.2
  91.9 9.1 %all-to-all-start.3 = ((bf16[32,100,128]{2,1,0:T(8,128)(2,1)}), bf16[32,100,128]{2,1,0:T(8,128)(2,1)}, u32[]{:S(2)}, u32[]{:S(2)}) async-start(bf16[32,100,128]{2,1,0:T(8,128)(2,1)} %broadcast_select_fusion), calls=%async_computation.3 | async-start | bytes 1703936 | tf_op jit(solution)/shard_map/all_to_all | solution.py:103
  101.1 2.6 reshape_reshape.4
  103.8 2.0 fusion.8
  105.8 25.4 %all-to-all-done.3 = bf16[32,100,128]{2,1,0:T(8,128)(2,1)} async-done(((bf16[32,100,128]{2,1,0:T(8,128)(2,1)}), bf16[32,100,128]{2,1,0:T(8,128)(2,1)}, u32[]{:S(2)}, u32[]{:S(2)}) %all-to-all-start.3) | async-done | bytes 819232 | tf_op jit(solution)/shard_map/all_to_all | solution.py:103
  131.2 1.4 copy.155
  133.9 18.3 %all-gather.3.cloned.1.call-done = bf16[4608,2048]{1,0:T(8,128)(2,1)} async-done(((bf16[288,2048]{1,0:T(8,128)(2,1)}), bf16[4608,2048]{1,0:T(8,128)(2,1)}) %all-gather.3.cloned.1.call-update) | async-done | bytes 18874384 | tf_op jit(solution)/shard_map/all_gather | solution.py:142
  152.1 9.7 %convolution_convert_fusion = bf16[256,2048]{1,0:T(8,128)(2,1)S(1)} fusion(bf16[256,4608]{1,0:T(8,128)(2,1)} %bitcast.124, bf16[4608,2048]{1,0:T(8,128)(2,1)} %all-gather.3.cloned.1.call-done), kind=kOutput, calls=%fused_computation.20 | convolution fusion | flops 4832362496 | bytes 22282240 | tf_op jit(solution)/shard_map/dot_general | solution.py:158
  162.8 2.0 copy.193
  164.9 2.0 copy.192
  166.9 3.0 fusion.46
  169.9 3.1 %fusion.15 = (f32[2,8,2,100]{3,2,1,0:T(2,128)S(1)}, f32[2,8,128,100,2]{2,3,4,1,0:T(8,128)S(1)}) fusion(f32[2,8,2,100,128]{4,3,2,1,0:T(8,128)} %get-tuple-element.32, f32[2,8,2,100]{3,2,1,0:T(2,128)S(1)} %get-tuple-element.31, bf16[2,128,8,128,1]{1,3,4,2,0:T(8,128)(2,1)} %bitcast.131, bf16[2,100,8,2,128]{4,1,3,2,0:T(8,128)(2,1)} %bitcast.129), kind=kOutput, calls=%fused_computation.25 | convolution fusion | flops 106083200 | bytes 4645888 | tf_op jit(solution)/shard_map/bakgd,blkd->bkgal/dot_general | solution.py:68
  174.1 1.5 fusion.23
  175.7 3.6 %copy.188 = bf16[2,100,8,2,128]{1,0,4,3,2:T(2,128)(2,1)} copy(bf16[2,100,8,2,128]{4,1,3,2,0:T(8,128)(2,1)} %fusion.23) | data formatting | bytes 1638400 | tf_op jit(solution)/shard_map/reshape | solution.py:85
  179.3 5.0 %all-to-all-start.4 = ((bf16[2,100,2048]{1,0,2:T(2,128)(2,1)}), bf16[2,100,2048]{1,0,2:T(2,128)(2,1)}, u32[]{:S(2)}, u32[]{:S(2)}) async-start(bf16[2,100,2048]{1,0,2:T(2,128)(2,1)} %bitcast.112), calls=%async_computation.4 | async-start | bytes 2097152 | tf_op jit(solution)/shard_map/all_to_all | solution.py:101
  184.3 3.2 %fusion.22 = bf16[2,100,8,2,128]{4,1,3,2,0:T(8,128)(2,1)} fusion(bf16[2,128,8,128,1]{1,3,4,2,0:T(8,128)(2,1)} %bitcast.132, f32[2,8,2,100,128]{4,3,2,1,0:T(8,128)} %get-tuple-element.32, f32[2,8,2,100]{3,2,1,0:T(2,128)S(1)} %get-tuple-element.31), kind=kOutput, calls=%fused_computation.37 | convolution fusion | flops 106086400 | bytes 2994688 | tf_op jit(solution)/shard_map/bkgal,blkd->bakgd/dot_general | solution.py:63
  187.5 3.7 %copy.181 = bf16[2,100,8,2,128]{1,0,4,3,2:T(2,128)(2,1)} copy(bf16[2,100,8,2,128]{4,1,3,2,0:T(8,128)(2,1)} %fusion.22) | data formatting | bytes 1638400 | tf_op jit(solution)/shard_map/reshape | solution.py:65
  191.2 16.0 %all-to-all-done.4 = bf16[2,100,2048]{1,0,2:T(2,128)(2,1)} async-done(((bf16[2,100,2048]{1,0,2:T(2,128)(2,1)}), bf16[2,100,2048]{1,0,2:T(2,128)(2,1)}, u32[]{:S(2)}, u32[]{:S(2)}) %all-to-all-start.4) | async-done | bytes 819232 | tf_op jit(solution)/shard_map/all_to_all | solution.py:101
  207.2 7.0 %all-to-all-start = ((bf16[2,100,2048]{1,0,2:T(2,128)(2,1)}), bf16[2,100,2048]{1,0,2:T(2,128)(2,1)}, u32[]{:S(2)}, u32[]{:S(2)}) async-start(bf16[2,100,2048]{1,0,2:T(2,128)(2,1)} %bitcast.111), calls=%async_computation | async-start | bytes 2097152 | tf_op jit(solution)/shard_map/all_to_all | solution.py:101
  214.3 3.5 %fusion.25 = bf16[2,8,128,128]{3,2,1,0:T(8,128)(2,1)} fusion(bf16[2,100,8,2,128]{4,1,3,2,0:T(8,128)(2,1)} %bitcast.130, f32[2,8,2,100,128]{4,3,2,1,0:T(8,128)} %get-tuple-element.32, f32[2,8,2,100]{3,2,1,0:T(2,128)S(1)} %get-tuple-element.31), kind=kOutput, calls=%fused_computation.40 | convolution fusion | flops 105938944 | bytes 2994688 | tf_op jit(solution)/shard_map/bkgal,bakgd->blkd/dot_general | solution.py:71
  217.8 2.1 copy.160
  219.9 2.4 fusion.24
  222.3 2.1 copy.159
  224.4 2.0 copy.189
  227.9 9.2 %all-to-all-done = bf16[2,100,2048]{1,0,2:T(2,128)(2,1)} async-done(((bf16[2,100,2048]{1,0,2:T(2,128)(2,1)}), bf16[2,100,2048]{1,0,2:T(2,128)(2,1)}, u32[]{:S(2)}, u32[]{:S(2)}) %all-to-all-start) | async-done | bytes 819232 | tf_op jit(solution)/shard_map/all_to_all | solution.py:101
  237.1 2.6 copy.182
  239.7 2.4 copy.147
  243.3 1.6 gather_fusion.3
  244.9 1.9 gather_fusion.1
  246.8 2.6 broadcast_select_fusion.1
  249.3 7.0 %all-to-all-start.1 = ((bf16[32,100,128]{2,1,0:T(8,128)(2,1)}), bf16[32,100,128]{2,1,0:T(8,128)(2,1)S(1)}, u32[]{:S(2)}, u32[]{:S(2)}) async-start(bf16[32,100,128]{2,1,0:T(8,128)(2,1)} %get-tuple-element.28), calls=%async_computation.1 | async-start | bytes 1703936 | tf_op jit(solution)/shard_map/all_to_all | solution.py:103
  256.4 11.0 %fusion.12 = (f32[2,128]{1,0:T(2,128)S(1)}, f32[2,128,4608]{2,1,0:T(8,128)}) fusion(bf16[2,128,4608]{2,1,0:T(8,128)(2,1)S(1)} %copy-done.2, f32[4608]{0:T(1024)S(1)} %copy-done.9, bf16[4608,2048]{1,0:T(8,128)(2,1)} %all-gather.3.cloned.1.call-done, bf16[2,128,1024]{2,1,0:T(8,128)(2,1)} %copy.160, bf16[2,128,1024]{2,1,0:T(8,128)(2,1)} %copy.159), kind=kOutput, calls=%fused_computation.18 | convolution fusion | flops 4838653952 | bytes 27020288 | tf_op jit(solution)/shard_map/dot_general | solution.py:164
  267.4 7.6 %all-to-all-done.1 = bf16[32,100,128]{2,1,0:T(8,128)(2,1)S(1)} async-done(((bf16[32,100,128]{2,1,0:T(8,128)(2,1)}), bf16[32,100,128]{2,1,0:T(8,128)(2,1)S(1)}, u32[]{:S(2)}, u32[]{:S(2)}) %all-to-all-start.1) | async-done | bytes 819232 | tf_op jit(solution)/shard_map/all_to_all | solution.py:103
  275.0 6.9 %all-to-all-start.5 = ((bf16[32,100,128]{2,1,0:T(8,128)(2,1)}), bf16[32,100,128]{2,1,0:T(8,128)(2,1)}, u32[]{:S(2)}, u32[]{:S(2)}) async-start(bf16[32,100,128]{2,1,0:T(8,128)(2,1)} %get-tuple-element.27), calls=%async_computation.5 | async-start | bytes 1703936 | tf_op jit(solution)/shard_map/all_to_all | solution.py:103
  282.0 5.2 %fusion.11 = bf16[2,128,4608]{2,1,0:T(8,128)(2,1)} fusion(bf16[2,128,4608]{2,1,0:T(8,128)(2,1)S(1)} %copy-done.2, f32[2,128,4608]{2,1,0:T(8,128)} %get-tuple-element.36, f32[2,128]{1,0:T(2,128)S(1)} %broadcast_multiply_fusion, f32[2,128]{1,0:T(2,128)S(1)} %get-tuple-element.25, f32[2,128]{1,0:T(2,128)S(1)} %get-tuple-element.26), kind=kLoop, calls=%fused_computation.17 | loop fusion | flops 7077888 | bytes 9440256 | tf_op jit(solution)/shard_map/convert_element_type | solution.py:171
  287.6 1.7 copy.168
  289.3 11.3 %all-to-all-done.5 = bf16[32,100,128]{2,1,0:T(8,128)(2,1)} async-done(((bf16[32,100,128]{2,1,0:T(8,128)(2,1)}), bf16[32,100,128]{2,1,0:T(8,128)(2,1)}, u32[]{:S(2)}, u32[]{:S(2)}) %all-to-all-start.5) | async-done | bytes 819232 | tf_op jit(solution)/shard_map/all_to_all | solution.py:103
  302.2 1.7 copy.169
  (77 shorter events, 15.7 us)
Async XLA Ops:
  7.2 67.6 %copy-start = (bf16[32,1024]{1,0:T(8,128)(2,1)S(1)}, bf16[32,1024]{1,0:T(8,128)(2,1)}, u32[]{:S(2)}) copy-start(bf16[32,1024]{1,0:T(8,128)(2,1)} %param.23) | copy-start | bytes 196612
  7.2 144.9 %all-gather.3.cloned.1.call-start = ((), (), s32[]{:S(2)}) async-start(), calls=%async_computation.6 | async-start | bytes 20054016 | tf_op jit(solution)/shard_map/all_gather | solution.py:142
  9.9 9.6 %copy-start.10 = (f32[2,2]{1,0:T(2,128)S(1)}, f32[2,2]{1,0:T(2,128)}, u32[]{:S(2)}) copy-start(f32[2,2]{1,0:T(2,128)} %param.21) | copy-start | bytes 52
  9.9 9.6 %copy-start.7 = (f32[2,2,50,32]{2,3,1,0:T(8,128)S(1)}, f32[2,2,50,32]{2,3,1,0:T(8,128)}, u32[]{:S(2)}) copy-start(f32[2,2,50,32]{2,3,1,0:T(8,128)} %param.19) | copy-start | bytes 76804
  9.9 9.6 %copy-start.8 = (f32[2,2,50,32]{2,3,1,0:T(8,128)S(1)}, f32[2,2,50,32]{2,3,1,0:T(8,128)}, u32[]{:S(2)}) copy-start(f32[2,2,50,32]{2,3,1,0:T(8,128)} %param.20) | copy-start | bytes 76804
  13.0 59.1 %copy-start.14 = (s32[32]{0:T(128)S(1)}, s32[32]{0:T(128)}, u32[]{:S(2)}) copy-start(s32[32]{0:T(128)} %param.18) | copy-start | bytes 388
  13.0 62.9 %copy-start.11 = (f32[1024]{0:T(1024)S(1)}, f32[1024]{0:T(1024)}, u32[]{:S(2)}) copy-start(f32[1024]{0:T(1024)} %param.22) | copy-start | bytes 12292
  13.0 70.9 %all-to-all-start.2 = ((bf16[2,100,2048]{1,0,2:T(2,128)(2,1)}), bf16[2,100,2048]{1,0,2:T(2,128)(2,1)S(1)}, u32[]{:S(2)}, u32[]{:S(2)}) async-start(bf16[2,100,2048]{1,0,2:T(2,128)(2,1)} %copy.151), calls=%async_computation.2 | async-start | bytes 2097152 | tf_op jit(solution)/shard_map/all_to_all | solution.py:101
  69.9 8.9 %copy-start.2 = (bf16[2,128,4608]{2,1,0:T(8,128)(2,1)S(1)}, bf16[2,128,4608]{2,1,0:T(8,128)(2,1)}, u32[]{:S(2)}) copy-start(bf16[2,128,4608]{2,1,0:T(8,128)(2,1)} %param.14) | copy-start | bytes 7077892
  72.2 0.5 copy-start.12
  74.6 4.1 %copy-start.13 = (s32[32]{0:T(128)S(1)}, s32[32]{0:T(128)}, u32[]{:S(2)}) copy-start(s32[32]{0:T(128)} %copy-done.12) | copy-start | bytes 388
  78.7 1.0 copy-start.6
  90.8 12.9 %copy-start.9 = (f32[4608]{0:T(1024)S(1)}, f32[4608]{0:T(1024)}, u32[]{:S(2)}) copy-start(f32[4608]{0:T(1024)} %param.15) | copy-start | bytes 55300
  91.9 39.3 %all-to-all-start.3 = ((bf16[32,100,128]{2,1,0:T(8,128)(2,1)}), bf16[32,100,128]{2,1,0:T(8,128)(2,1)}, u32[]{:S(2)}, u32[]{:S(2)}) async-start(bf16[32,100,128]{2,1,0:T(8,128)(2,1)} %broadcast_select_fusion), calls=%async_computation.3 | async-start | bytes 1703936 | tf_op jit(solution)/shard_map/all_to_all | solution.py:103
  103.7 63.2 %copy-start.3 = (bf16[2,100,8,2,128]{4,3,2,1,0:T(2,128)(2,1)}, bf16[2,100,8,2,128]{4,3,2,1,0:T(2,128)(2,1)S(1)}, u32[]{:S(2)}) copy-start(bf16[2,100,8,2,128]{4,3,2,1,0:T(2,128)(2,1)S(1)} %reshape_reshape.4) | copy-start | bytes 2457604
  169.9 3.2 %copy-start.5 = (f32[2,8,2,100,128]{4,3,2,1,0:T(8,128)S(1)}, f32[2,8,2,100,128]{4,3,2,1,0:T(8,128)}, u32[]{:S(2)}) copy-start(f32[2,8,2,100,128]{4,3,2,1,0:T(8,128)} %get-tuple-element.32) | copy-start | bytes 4915204
  173.0 1.1 copy-start.4
  179.3 27.9 %all-to-all-start.4 = ((bf16[2,100,2048]{1,0,2:T(2,128)(2,1)}), bf16[2,100,2048]{1,0,2:T(2,128)(2,1)}, u32[]{:S(2)}, u32[]{:S(2)}) async-start(bf16[2,100,2048]{1,0,2:T(2,128)(2,1)} %bitcast.112), calls=%async_computation.4 | async-start | bytes 2097152 | tf_op jit(solution)/shard_map/all_to_all | solution.py:101
  187.5 26.7 %copy-start.15 = (s32[32]{0:T(128)S(1)}, s32[32]{0:T(128)}, u32[]{:S(2)}) copy-start(s32[32]{0:T(128)} %param.18) | copy-start | bytes 388
  207.2 29.9 %all-to-all-start = ((bf16[2,100,2048]{1,0,2:T(2,128)(2,1)}), bf16[2,100,2048]{1,0,2:T(2,128)(2,1)}, u32[]{:S(2)}, u32[]{:S(2)}) async-start(bf16[2,100,2048]{1,0,2:T(2,128)(2,1)} %bitcast.111), calls=%async_computation | async-start | bytes 2097152 | tf_op jit(solution)/shard_map/all_to_all | solution.py:101
  249.3 25.7 %all-to-all-start.1 = ((bf16[32,100,128]{2,1,0:T(8,128)(2,1)}), bf16[32,100,128]{2,1,0:T(8,128)(2,1)S(1)}, u32[]{:S(2)}, u32[]{:S(2)}) async-start(bf16[32,100,128]{2,1,0:T(8,128)(2,1)} %get-tuple-element.28), calls=%async_computation.1 | async-start | bytes 1703936 | tf_op jit(solution)/shard_map/all_to_all | solution.py:103
  275.0 25.6 %all-to-all-start.5 = ((bf16[32,100,128]{2,1,0:T(8,128)(2,1)}), bf16[32,100,128]{2,1,0:T(8,128)(2,1)}, u32[]{:S(2)}, u32[]{:S(2)}) async-start(bf16[32,100,128]{2,1,0:T(8,128)(2,1)} %get-tuple-element.27), calls=%async_computation.5 | async-start | bytes 1703936 | tf_op jit(solution)/shard_map/all_to_all | solution.py:103
  300.6 3.3 %copy-start.1 = (bf16[32,1024]{1,0:T(8,128)(2,1)S(1)}, bf16[32,1024]{1,0:T(8,128)(2,1)}, u32[]{:S(2)}) copy-start(bf16[32,1024]{1,0:T(8,128)(2,1)} %param.23) | copy-start | bytes 196612
Sparse Core Ops, SparseCore 0:
  9.6 142.4 all-gather.2

commit v2 on v0

--- a/solution.py
+++ b/solution.py
@@ -1,8 +1,11 @@
+import functools
 import math
 
 import jax
 import jax.numpy as jnp
 from jax import lax
+from jax.experimental import pallas as pl
+from jax.experimental.pallas import tpu as pltpu
 from jax.sharding import PartitionSpec as P
 
 KV_HEADS = 8
@@ -107,6 +110,224 @@
     spread = lax.all_to_all(block, "seq", split_axis=2, concat_axis=0, tiled=True)
     arranged = jnp.take(spread, ordering, axis=0)
     return lax.all_to_all(arranged, "seq", split_axis=0, concat_axis=2, tiled=True)
+
+
+def exchange_kernel(
+    n,
+    order_ref,
+    inverse_ref,
+    length_ref,
+    keyval_ref,
+    query_ref,
+    upstream_ref,
+    attended_ref,
+    grad_query_ref,
+    restored_ref,
+    owned,
+    spread,
+    arranged,
+    grads,
+    spread_back,
+    arranged_back,
+    send_sems,
+    recv_sems,
+    local_sems,
+):
+    me = lax.axis_index("seq")
+    own = keyval_ref.shape[0]
+    heads = KV_HEADS
+    episodes = spread.shape[0]
+
+    def columns(index):
+        return pl.ds(pl.multiple_of(index * HEAD, HEAD), HEAD)
+
+    def rows(index):
+        return pl.ds(index * own, own)
+
+    def remote(stage, source, target, device, origin):
+        return pltpu.make_async_remote_copy(
+            src_ref=source,
+            dst_ref=target,
+            send_sem=send_sems.at[stage, device],
+            recv_sem=recv_sems.at[stage, origin],
+            device_id={"seq": device},
+            device_id_type=pl.DeviceIdType.MESH,
+        )
+
+    def others(body):
+        def step(k, carry):
+            body(lax.rem(me + k, n))
+            return carry
+
+        lax.fori_loop(1, n, step, 0)
+
+    barrier = pltpu.get_barrier_semaphore()
+    others(
+        lambda d: pl.semaphore_signal(
+            barrier, inc=1, device_id={"seq": d}, device_id_type=pl.DeviceIdType.MESH
+        )
+    )
+    pl.semaphore_wait(barrier, n - 1)
+
+    def first(d):
+        return remote(0, keyval_ref.at[:, :, columns(d)], spread.at[rows(me)], d, me)
+
+    def first_in(d):
+        return remote(0, keyval_ref.at[:, :, columns(d)], spread.at[rows(d)], d, d)
+
+    kept = pltpu.make_async_copy(
+        keyval_ref.at[:, :, columns(me)], spread.at[rows(me)], local_sems.at[0]
+    )
+    kept.start()
+    others(lambda d: first(d).start())
+    kept.wait()
+    others(lambda d: first_in(d).wait_recv())
+
+    def arrange(source, target, order):
+        def step(e, carry):
+            target[e] = source[order[e]]
+            return carry
+
+        lax.fori_loop(0, episodes, step, 0)
+
+    arrange(spread, arranged, order_ref)
+
+    def second(d):
+        return remote(1, arranged.at[rows(d)], owned.at[:, :, columns(me)], d, me)
+
+    def second_in(d):
+        return remote(1, arranged.at[rows(d)], owned.at[:, :, columns(d)], d, d)
+
+    kept = pltpu.make_async_copy(
+        arranged.at[rows(me)], owned.at[:, :, columns(me)], local_sems.at[1]
+    )
+    kept.start()
+    others(lambda d: second(d).start())
+    kept.wait()
+
+    def third(d):
+        return remote(2, grads.at[:, :, columns(d)], spread_back.at[rows(me)], d, me)
+
+    def third_in(d):
+        return remote(2, grads.at[:, :, columns(d)], spread_back.at[rows(d)], d, d)
+
+    def head(h, carry):
+        for d in (h, h + heads):
+            @pl.when(d != me)
+            def _():
+                second_in(d).wait_recv()
+
+        even, odd = columns(2 * h), columns(2 * h + 1)
+        for s in range(own):
+            keys = owned[s, :, columns(h)]
+            values = owned[s, :, columns(h + heads)]
+            query = jnp.concatenate([query_ref[s, :, even], query_ref[s, :, odd]], axis=0)
+            upstream = jnp.concatenate(
+                [upstream_ref[s, :, even], upstream_ref[s, :, odd]], axis=0
+            )
+            half = query.shape[0] // 2
+            scores = lax.dot_general(
+                query, keys, (((1,), (1,)), ((), ())), preferred_element_type=jnp.float32
+            )
+            visible = lax.broadcasted_iota(jnp.int32, scores.shape, 1) < length_ref[s]
+            masked = jnp.where(visible, scores, -1e30)
+            exps = jnp.where(
+                visible, jnp.exp(masked - jnp.max(masked, axis=-1, keepdims=True)), 0.0
+            )
+            probabilities = exps / jnp.sum(exps, axis=-1, keepdims=True)
+            rounded = probabilities.astype(jnp.bfloat16)
+            attended = jnp.dot(rounded, values, preferred_element_type=jnp.float32)
+            grad_prob = lax.dot_general(
+                upstream, values, (((1,), (1,)), ((), ())), preferred_element_type=jnp.float32
+            )
+            grad_value = lax.dot_general(
+                rounded, upstream, (((0,), (0,)), ((), ())), preferred_element_type=jnp.float32
+            )
+            grad_score = (
+                probabilities
+                * (grad_prob - jnp.sum(grad_prob * probabilities, axis=-1, keepdims=True))
+            ).astype(jnp.bfloat16)
+            grad_query = (
+                jnp.dot(grad_score, keys, preferred_element_type=jnp.float32) * HEAD ** (-0.5)
+            )
+            grad_key = lax.dot_general(
+                grad_score, query, (((0,), (0,)), ((), ())), preferred_element_type=jnp.float32
+            )
+            attended_ref[s, :, even] = attended[:half].astype(jnp.bfloat16)
+            attended_ref[s, :, odd] = attended[half:].astype(jnp.bfloat16)
+            grad_query_ref[s, :, even] = grad_query[:half].astype(jnp.bfloat16)
+            grad_query_ref[s, :, odd] = grad_query[half:].astype(jnp.bfloat16)
+            grads[s, :, columns(h)] = grad_key.astype(jnp.bfloat16)
+            grads[s, :, columns(h + heads)] = grad_value.astype(jnp.bfloat16)
+        for d in (h, h + heads):
+            @pl.when(d != me)
+            def _():
+                third(d).start()
+        return carry
+
+    lax.fori_loop(0, heads, head, 0)
+
+    kept = pltpu.make_async_copy(
+        grads.at[:, :, columns(me)], spread_back.at[rows(me)], local_sems.at[2]
+    )
+    kept.start()
+    kept.wait()
+    others(lambda d: third_in(d).wait_recv())
+    arrange(spread_back, arranged_back, inverse_ref)
+
+    def fourth(d):
+        return remote(3, arranged_back.at[rows(d)], restored_ref.at[:, :, columns(me)], d, me)
+
+    def fourth_in(d):
+        return remote(3, arranged_back.at[rows(d)], restored_ref.at[:, :, columns(d)], d, d)
+
+    kept = pltpu.make_async_copy(
+        arranged_back.at[rows(me)], restored_ref.at[:, :, columns(me)], local_sems.at[3]
+    )
+    kept.start()
+    others(lambda d: fourth(d).start())
+    kept.wait()
+    others(lambda d: fourth_in(d).wait_recv())
+
+    def sent(d):
+        first(d).wait_send()
+        second(d).wait_send()
+        third(d).wait_send()
+        fourth(d).wait_send()
+
+    others(sent)
+
+
+def exchange(assign, inverse, owned_len, keyval, queries, upstream):
+    n = lax.axis_size("seq")
+    owned_count, positions, doubled = keyval.shape
+    episodes = assign.shape[0]
+    padded = jax.ShapeDtypeStruct(queries.shape, jnp.bfloat16)
+    blocks = pltpu.VMEM((episodes, positions, HEAD), jnp.bfloat16)
+    whole = pltpu.VMEM(keyval.shape, jnp.bfloat16)
+    memory = pl.BlockSpec(memory_space=pltpu.VMEM)
+    scalars = pl.BlockSpec(memory_space=pltpu.SMEM)
+    return pl.pallas_call(
+        functools.partial(exchange_kernel, n),
+        out_shape=(padded, padded, jax.ShapeDtypeStruct(keyval.shape, jnp.bfloat16)),
+        in_specs=[scalars] * 3 + [memory] * 3,
+        out_specs=(memory,) * 3,
+        scratch_shapes=[
+            whole,
+            blocks,
+            blocks,
+            whole,
+            blocks,
+            blocks,
+            pltpu.SemaphoreType.DMA((4, n)),
+            pltpu.SemaphoreType.DMA((4, n)),
+            pltpu.SemaphoreType.DMA((4,)),
+        ],
+        compiler_params=pltpu.CompilerParams(
+            collective_id=0, has_side_effects=True, vmem_limit_bytes=40 * 2**20
+        ),
+        name="exchange",
+    )(assign, inverse, owned_len, keyval, queries, upstream)
 
 
 def shards(
@@ -152,9 +373,17 @@
     my_slots = lax.dynamic_slice_in_dim(assign, position * owned_count, owned_count)
     chosen = slot_index[None, :] == my_slots[:, None]
     owned_len = jnp.sum(jnp.where(chosen, lengths[None, :], 0), axis=1)
-    owned_kv = route_keys(keyval, assign)
-    attended, grad_kv, grad_query = attend(queries, owned_kv, owned_len, upstream, KV_HEADS)
-    grad_keyval = route_keys(grad_kv, inverse)
+    if doubled // lax.axis_size("seq") == HEAD:
+        row_count = samples * horizon
+        extra = ((0, 0), (0, positions - row_count), (0, 0))
+        attended, grad_query, grad_keyval = exchange(
+            assign, inverse, owned_len, keyval, jnp.pad(queries, extra), jnp.pad(upstream, extra)
+        )
+        attended, grad_query = attended[:, :row_count], grad_query[:, :row_count]
+    else:
+        owned_kv = route_keys(keyval, assign)
+        attended, grad_kv, grad_query = attend(queries, owned_kv, owned_len, upstream, KV_HEADS)
+        grad_keyval = route_keys(grad_kv, inverse)
     restored = grad_keyval.reshape(owned_count * positions, doubled)
     grad_normed = lax.dot_general(
         restored, whole_weight, (((1,), (1,)), ((), ())), preferred_element_type=jnp.float32

time: 303 us -> 245 us (0.81)
  Pallas kernels: 0 us -> 99.5 us
  waiting for transfers between devices: 152 us -> 88 us
  local copies, waits for them, and re-layouts: 44 us -> 7.78 us
  starting transfers between devices: 26.3 us -> 0.04 us
  other arithmetic: 27 us -> 11.5 us
  matrix products: 35.9 us -> 23.2 us
    pallas_call x0 -> x1, Pallas kernels: none -> 99.5 us  [exchange(): pl.pallas_call(functools.partial(exchange_kernel, n), out_shape=(padded,...]
    all_to_all x4 -> x0, waiting for transfers between devices: 53.5 us -> none  [the longest x2 37.2 us: route_keys(): lax.all_to_all(block, 'seq', split_axis=2, concat_axis=0, tiled=True)]
    all_to_all x4 -> x0, starting transfers between devices: 26.2 us -> none  [the longest x2 14 us: route_keys(): lax.all_to_all(arranged, 'seq', split_axis=0, concat_axis=2, tiled=True)]
    another operation x4 -> x0, local copies, waits for them, and re-layouts: 11.9 us -> none  [the longest x1 3.79 us: attend(): upstream.reshape(batch_count, row_count, kv_heads, group_size, head_dim)]
    concatenate x1 -> x0, other arithmetic: 10.3 us -> none  [attend(): jnp.concatenate([grad_key.reshape(batch_count, positions, kv_width), grad...]
    all_gather x1, waiting for transfers between devices: 97.7 us -> 87.3 us  [shards(): whole_weight = lax.all_gather(kv_weight, 'seq', axis=0, tiled=True)]
    all_to_all x5 -> x0, local copies, waits for them, and re-layouts: 9.32 us -> none  [the longest x4 8.02 us: route_keys(): lax.all_to_all(block, 'seq', split_axis=2, concat_axis=0, tiled=True)]
    dot_general x5 -> x0, matrix products: 8.6 us -> none  [the longest x1 2.84 us: attend(): jnp.einsum('bkgal,bakgd->blkd', rounded, upstream_heads, preferred_elemen...]
  transfers between devices with their start and end apart: 5 -> 1, of which waited for: 5 -> 1; matrix products, arithmetic and copies ran while one was open for 14% -> 6% of each run, Pallas kernels for 0% -> 0%
where the time goes in v2:
time: 245 us; the launch traced here: 244 us
  Pallas kernels  99.5 us (41%)
  waiting for transfers between devices  88 us (36%)
  matrix products  23.2 us (9%)
  between operations  14.3 us (6%)
  other arithmetic  11.5 us (5%)
  local copies, waits for them, and re-layouts  7.78 us (3%)
    pallas_call x1, Pallas kernels, exchange(): pl.pallas_call(functools.partial(exchange_kernel, n), out_shape=(padded,...  99.5 us
    all_gather x1, waiting for transfers between devices, shards(): whole_weight = lax.all_gather(kv_weight, 'seq', axis=0, tiled=True)  87.3 us
    dot_general x1, matrix products, shards(): lax.dot_general(restored, whole_weight, (((1,), (1,)), ((), ())), preferr...  9.91 us
    dot_general x1, matrix products, shards(): product = jnp.dot(normed, whole_weight, preferred_element_type=jnp.float32)  9.66 us
  transfers between devices with their start and end apart: 1, of which 1 were waited for; matrix products, arithmetic and copies ran while one was open for 6% of the time, Pallas kernels for 0%

profile of v2, /device:TPU:21, one launch (start us, length us, event | category | flops | bytes accessed | tf_op | source)
XLA Modules:
  0.0 244.3 jit_solution(1421459705519084604)
XLA Ops:
  7.2 0.0 copy-start
  7.2 0.0 all-gather.2.cloned.1.call-start
  7.2 0.7 all-gather.2.cloned.1.call-update
  7.9 0.8 mul.130
  8.7 0.1 multiply_sine_fusion
  8.9 1.0 fusion.15
  9.8 0.0 copy-done
  9.8 0.4 multiply_reduce_fusion
  10.2 0.0 copy-start.3
  10.2 0.9 multiply_convert_fusion
  11.2 0.1 reshape.112
  11.3 3.2 %fusion.12 = bf16[200,2048]{1,0:T(8,128)(2,1)S(1)} fusion(bf16[200,1024]{1,0:T(8,128)(2,1)S(1)} %reshape.112, bf16[1024,2048]{1,0:T(8,128)(2,1)} %param.22), kind=kOutput, calls=%fused_computation.16 | convolution fusion | flops 839680000 | bytes 5423104 | tf_op jit(solution)/shard_map/dot_general | solution.py:45
  14.5 0.0 copy-start.1
  14.5 0.0 copy-start.5
  14.5 0.2 reshape.113
  14.7 0.0 copy-done.3
  14.7 0.0 copy-start.4
  14.7 0.8 copy.24
  15.6 0.3 copy.25
  15.8 0.1 pad.7.query_ref
  15.9 0.1 pad.8.upstream_ref
  16.1 0.0 copy-done.1
  16.1 0.1 dynamic_slice.3
  16.1 0.1 select_reduce_fusion.inverse_ref
  16.3 0.0 copy-done.5
  16.3 0.2 fusion.16.length_ref
  16.4 2.3 fusion.5
  18.8 0.0 copy-done.4
  18.8 3.7 %fusion.7 = bf16[2,128,4608]{2,1,0:T(8,128)(2,1)} fusion(bf16[2,128,4608]{2,1,0:T(8,128)(2,1)} %param.12, f32[4608]{0:T(1024)S(1)} %copy-done.4, f32[2,128]{1,0:T(2,128)S(1)} %get-tuple-element.21), kind=kLoop, calls=%fused_computation.9 | loop fusion | flops 4718592 | bytes 4738048 | tf_op jit(solution)/shard_map/convert_element_type | solution.py:360
  22.5 87.3 %all-gather.2.cloned.1.call-done = bf16[4608,2048]{1,0:T(8,128)(2,1)} async-done(((bf16[288,2048]{1,0:T(8,128)(2,1)}), bf16[4608,2048]{1,0:T(8,128)(2,1)}) %all-gather.2.cloned.1.call-update) | async-done | bytes 18874384 | tf_op jit(solution)/shard_map/all_gather | solution.py:363
  109.8 9.7 %convolution_convert_fusion = bf16[256,2048]{1,0:T(8,128)(2,1)S(1)} fusion(bf16[256,4608]{1,0:T(8,128)(2,1)} %bitcast.37, bf16[4608,2048]{1,0:T(8,128)(2,1)} %all-gather.2.cloned.1.call-done), kind=kOutput, calls=%fused_computation.15 | convolution fusion | flops 4832362496 | bytes 22282240 | tf_op jit(solution)/shard_map/dot_general | solution.py:364
  119.5 99.5 %exchange.1 = (bf16[2,128,2048]{2,1,0:T(8,128)(2,1)S(1)}, bf16[2,128,2048]{2,1,0:T(8,128)(2,1)S(1)}, bf16[2,128,2048]{2,1,0:T(8,128)(2,1)S(1)}) custom-call(s32[32]{0:T(128)S(1)} %copy-done.1, s32[32]{0:T(128)S(1)} %select_reduce_fusion.inverse_ref, s32[2]{0:T(128)S(1)} %fusion.16.length_ref, bf16[2,128,2048]{2,1,0:T(8,128)(2,1)S(1)} %bitcast.33, ...), custom_call_target="tpu_custom_call" | custom-call | tf_op jit(solution)/shard_map/exchange/pallas_call | solution.py:310
  219.0 0.1 slice.6
  219.1 0.8 copy.26
  219.9 1.7 copy.28
  221.7 9.9 %fusion.11 = (f32[2,128]{1,0:T(2,128)S(1)}, f32[2,128,4608]{2,1,0:T(8,128)S(1)}) fusion(bf16[2,128,4608]{2,1,0:T(8,128)(2,1)} %param.12, f32[4608]{0:T(1024)S(1)} %copy-done.4, bf16[2,128,2048]{2,1,0:T(8,128)(2,1)S(1)} %get-tuple-element.7, bf16[4608,2048]{1,0:T(8,128)(2,1)} %all-gather.2.cloned.1.call-done), kind=kOutput, calls=%fused_computation.13 | convolution fusion | flops 4836556800 | bytes 27020288 | tf_op jit(solution)/shard_map/dot_general | solution.py:388
  231.6 0.0 copy-start.2
  231.6 0.1 slice.7
  231.7 0.8 copy.27
  232.6 1.7 copy.29
  234.3 0.0 copy-done.2
  234.3 3.1 %fusion.10 = bf16[2,128,4608]{2,1,0:T(8,128)(2,1)} fusion(bf16[2,128,4608]{2,1,0:T(8,128)(2,1)S(1)} %copy-done.2, f32[2,128,4608]{2,1,0:T(8,128)S(1)} %get-tuple-element.27, f32[2,128]{1,0:T(2,128)S(1)} %broadcast_multiply_fusion, f32[2,128]{1,0:T(2,128)S(1)} %get-tuple-element.20, f32[2,128]{1,0:T(2,128)S(1)} %get-tuple-element.21), kind=kLoop, calls=%fused_computation.12 | loop fusion | flops 7077888 | bytes 9440256 | tf_op jit(solution)/shard_map/convert_element_type | solution.py:395
  (6 shorter events, 0.0 us)
Async XLA Ops:
  7.2 2.7 %copy-start = (bf16[32,1024]{1,0:T(8,128)(2,1)S(1)}, bf16[32,1024]{1,0:T(8,128)(2,1)}, u32[]{:S(2)}) copy-start(bf16[32,1024]{1,0:T(8,128)(2,1)} %param.21) | copy-start | bytes 196612
  7.2 102.7 %all-gather.2.cloned.1.call-start = ((), (), s32[]{:S(2)}) async-start(), calls=%async_computation | async-start | bytes 20054016 | tf_op jit(solution)/shard_map/all_gather | solution.py:363
  10.2 4.5 %copy-start.3 = (bf16[2,2,50,2048]{3,1,2,0:T(2,128)(2,1)S(1)}, bf16[2,2,50,2048]{3,1,2,0:T(2,128)(2,1)}, u32[]{:S(2)}) copy-start(bf16[2,2,50,2048]{3,1,2,0:T(2,128)(2,1)} %param.23) | copy-start | bytes 2457604
  14.5 1.6 copy-start.1
  14.5 1.8 copy-start.5
  14.7 4.1 %copy-start.4 = (f32[4608]{0:T(1024)S(1)}, f32[4608]{0:T(1024)}, u32[]{:S(2)}) copy-start(f32[4608]{0:T(1024)} %param.13) | copy-start | bytes 55300
  231.6 2.7 %copy-start.2 = (bf16[2,128,4608]{2,1,0:T(8,128)(2,1)S(1)}, bf16[2,128,4608]{2,1,0:T(8,128)(2,1)}, u32[]{:S(2)}) copy-start(bf16[2,128,4608]{2,1,0:T(8,128)(2,1)} %param.12) | copy-start | bytes 7077892
Sparse Core Ops, SparseCore 0:
  9.6 100.1 all-gather.1

commit v3 on v2

--- a/solution.py
+++ b/solution.py
@@ -330,6 +330,223 @@
     )(assign, inverse, owned_len, keyval, queries, upstream)
 
 
+def gather_kernel(
+    n,
+    weight_ref,
+    normed_ref,
+    whole_ref,
+    keyval_ref,
+    held,
+    total,
+    ring_send,
+    ring_recv,
+    pair_send,
+    pair_recv,
+    cross_send,
+    cross_recv,
+    start_send,
+    start_recv,
+    out_sems,
+):
+    chips = n // 2
+    part = lax.axis_index("parts")
+    me = lax.axis_index("seq")
+    chip, core = me // 2, lax.rem(me, 2)
+    depth_place, side = chip // 2, lax.rem(chip, 2)
+    place = depth_place + side * (chips - 1 - 2 * depth_place)
+    width = held.shape[2]
+    quarter, half, piece = width // 4, width // 2, width // 16
+
+    def chip_at(position):
+        position = lax.rem(position + 2 * chips, chips)
+        return jnp.where(position < chips // 2, 2 * position, 2 * (chips - 1 - position) + 1)
+
+    def span(start, size):
+        return pl.ds(pl.multiple_of(start, piece), size)
+
+    def columns(which, kind):
+        if kind == 0:
+            return span(which * quarter, 2 * piece)
+        own = part if kind == 1 else 1 - part
+        return span(which * quarter + (2 + own) * piece, piece)
+
+    def rows(of):
+        return pl.ds(of * 2, 2)
+
+    def arriving(d, s):
+        return chip_at(place - 1 - s if d == 0 else place + 1 + s)
+
+    def leaving(d, s):
+        return chip_at(place - s if d == 0 else place + s)
+
+    def send(ref, device, send_sem, recv_sem):
+        return pltpu.make_async_remote_copy(
+            src_ref=ref,
+            dst_ref=ref,
+            send_sem=send_sem,
+            recv_sem=recv_sem,
+            device_id=device,
+            device_id_type=pl.DeviceIdType.MESH,
+        )
+
+    onward = [{"seq": chip_at(place + 1) * 2 + core}, {"seq": chip_at(place - 1) * 2 + core}]
+    sibling = {"seq": chip * 2 + 1 - core}
+    opposite = {"parts": 1 - part, "seq": me}
+
+    def ring(d, kind, s, of):
+        ref = held.at[rows(of), :, columns(core * 2 + d, kind)]
+        return send(ref, onward[d], ring_send.at[d, kind, s], ring_recv.at[d, kind, s])
+
+    def pair(d, kind, s, whose):
+        ref = held.at[rows(arriving(d, s)), :, columns(whose * 2 + d, kind)]
+        return send(ref, sibling, pair_send.at[d, kind, s], pair_recv.at[d, kind, s])
+
+    def cross(d, kind, s):
+        ref = held.at[rows(arriving(d, s)), :, columns(core * 2 + d, kind)]
+        return send(ref, opposite, cross_send.at[d, s], cross_recv.at[d, s])
+
+    def start(k, shard, whose):
+        ref = held.at[shard, :, span(whose * half, half)]
+        return send(ref, sibling, start_send.at[k], start_recv.at[k])
+
+    barrier = pltpu.get_barrier_semaphore()
+    for device in (*onward, sibling, opposite):
+        pl.semaphore_signal(
+            barrier, inc=1, device_id=device, device_id_type=pl.DeviceIdType.MESH
+        )
+    mine = pltpu.make_async_copy(weight_ref, held.at[me], out_sems.at[0, 0, chips])
+    mine.start()
+    mine.wait()
+    pl.semaphore_wait(barrier, 4)
+
+    start(0, me, 1 - core).start()
+    start(1, me, core).start()
+    other = chip * 2 + 1 - core
+    start(0, other, core).wait_recv()
+    for kind in (0, 1):
+        for d in (0, 1):
+            ring(d, kind, 0, chip).start()
+    start(1, other, 1 - core).wait_recv()
+
+    def product(of, which):
+        cols = span(which * quarter, quarter)
+        return jnp.dot(
+            normed_ref[of * 2], held[of * 2, :, cols], preferred_element_type=jnp.float32
+        ) + jnp.dot(
+            normed_ref[of * 2 + 1], held[of * 2 + 1, :, cols], preferred_element_type=jnp.float32
+        )
+
+    def write(of, which, index):
+        at = (rows(of), slice(None), span(which * quarter, quarter))
+        return pltpu.make_async_copy(
+            held.at[at], whole_ref.at[at], out_sems.at[which // 2, lax.rem(which, 2), index]
+        )
+
+    def own(which, carry):
+        write(chip, which, chips - 1).start()
+        total[:, span(which * quarter, quarter)] = product(chip, which)
+        return carry
+
+    lax.fori_loop(0, 4, own, 0)
+
+    def step(s, carry):
+        @pl.when(s <= chips - 2)
+        def _():
+            for kind in (0, 1):
+                for d in (0, 1):
+                    ring(d, kind, s, arriving(d, s)).wait_recv()
+
+                    @pl.when(s < chips - 2)
+                    def _():
+                        ring(d, kind, s + 1, arriving(d, s)).start()
+
+                    pair(d, kind, s, core).start()
+                    if kind == 1:
+                        cross(d, 1, s).start()
+
+        @pl.when((s >= 1) & (s <= chips - 1))
+        def _():
+            for d in (0, 1):
+                cross(d, 2, s - 1).wait_recv()
+                pair(d, 2, s - 1, core).start()
+
+        @pl.when(s >= 2)
+        def _():
+            for d in (0, 1):
+                for kind in (0, 1, 2):
+                    pair(d, kind, s - 2, 1 - core).wait_recv()
+                of = arriving(d, s - 2)
+                for which in (d, 2 + d):
+                    write(of, which, s - 2).start()
+                    total[:, span(which * quarter, quarter)] += product(of, which)
+
+        return carry
+
+    lax.fori_loop(0, chips + 1, step, 0)
+    keyval_ref[...] = total[...].astype(keyval_ref.dtype)
+
+    start(0, me, 1 - core).wait_send()
+    start(1, me, core).wait_send()
+
+    def finish(s, carry):
+        for d in (0, 1):
+            for kind in (0, 1):
+                ring(d, kind, s, leaving(d, s)).wait_send()
+            for kind in (0, 1, 2):
+                pair(d, kind, s, core).wait_send()
+            cross(d, 1, s).wait_send()
+            for which in (d, 2 + d):
+                write(arriving(d, s), which, s).wait()
+        return carry
+
+    lax.fori_loop(0, chips - 1, finish, 0)
+    for which in range(4):
+        write(chip, which, chips - 1).wait()
+
+
+def gather_project(kv_weight, normed):
+    n = lax.axis_size("seq")
+    chips = n // 2
+    depth, doubled = kv_weight.shape
+    tokens = normed.shape[0]
+    parted = normed.reshape(tokens, n, depth).transpose(1, 0, 2)
+    steps = chips - 1
+    sems = pltpu.SemaphoreType.DMA
+    whole, keyval = pl.pallas_call(
+        functools.partial(gather_kernel, n),
+        out_shape=(
+            jax.ShapeDtypeStruct((n, depth, doubled), jnp.bfloat16),
+            jax.ShapeDtypeStruct((tokens, doubled), jnp.bfloat16),
+        ),
+        in_specs=[
+            pl.BlockSpec(memory_space=pl.ANY),
+            pl.BlockSpec(memory_space=pltpu.VMEM),
+        ],
+        out_specs=(
+            pl.BlockSpec(memory_space=pl.ANY),
+            pl.BlockSpec(memory_space=pltpu.VMEM),
+        ),
+        scratch_shapes=[
+            pltpu.VMEM((n, depth, doubled), jnp.bfloat16),
+            pltpu.VMEM((tokens, doubled), jnp.float32),
+            sems((2, 2, steps)),
+            sems((2, 2, steps)),
+            sems((2, 3, steps)),
+            sems((2, 3, steps)),
+            sems((2, steps)),
+            sems((2, steps)),
+            sems((2,)),
+            sems((2,)),
+            sems((2, 2, chips + 1)),
+        ],
+        compiler_params=pltpu.CompilerParams(
+            collective_id=1, has_side_effects=True, vmem_limit_bytes=48 * 2**20
+        ),
+        name="gather_project",
+    )(kv_weight, parted)
+    return whole.reshape(n * depth, doubled), keyval
+
+
 def shards(
     prefix,
     backbone_gain,
@@ -360,8 +577,13 @@
         .astype(jnp.bfloat16)
         .reshape(owned_count * positions, model_width)
     )
-    whole_weight = lax.all_gather(kv_weight, "seq", axis=0, tiled=True)
-    product = jnp.dot(normed, whole_weight, preferred_element_type=jnp.float32)
+    n = lax.axis_size("seq")
+    fits = doubled // n == HEAD and kv_weight.shape[0] % 16 == 0
+    if fits and n % 4 == 0 and lax.axis_size("parts") == 2:
+        whole_weight, product = gather_project(kv_weight, normed)
+    else:
+        whole_weight = lax.all_gather(kv_weight, "seq", axis=0, tiled=True)
+        product = jnp.dot(normed, whole_weight, preferred_element_type=jnp.float32)
     keyval = product.astype(jnp.bfloat16).reshape(owned_count, positions, doubled)
     queries = expert_queries(
         actions, flow_noise, timesteps, expert_gain, action_weight, query_weight, HEAD
@@ -373,7 +595,7 @@
     my_slots = lax.dynamic_slice_in_dim(assign, position * owned_count, owned_count)
     chosen = slot_index[None, :] == my_slots[:, None]
     owned_len = jnp.sum(jnp.where(chosen, lengths[None, :], 0), axis=1)
-    if doubled // lax.axis_size("seq") == HEAD:
+    if doubled // n == HEAD:
         row_count = samples * horizon
         extra = ((0, 0), (0, positions - row_count), (0, 0))
         attended, grad_query, grad_keyval = exchange(

time: 245 us -> 237 us (0.967)
  Pallas kernels: 99.5 us -> 191 us
  waiting for transfers between devices: 88 us -> 0 us
  between operations: 14.3 us -> 0.88 us
  local copies, waits for them, and re-layouts: 7.78 us -> 19.2 us
  matrix products: 23.2 us -> 13.8 us
    all_gather x1 -> x0, waiting for transfers between devices: 87.3 us -> none  [shards(): whole_weight = lax.all_gather(kv_weight, 'seq', axis=0, tiled=True)]
    pallas_call x0 -> x1, Pallas kernels: none -> 84.8 us  [gather_project(): pl.pallas_call(functools.partial(gather_kernel, n), out_shape=(jax.ShapeD...]
    dot_general x1 -> x0, matrix products: 9.66 us -> none  [shards(): product = jnp.dot(normed, whole_weight, preferred_element_type=jnp.float32)]
    another operation x0 -> x2, local copies, waits for them, and re-layouts: none -> 9.58 us  [gather_project(): parted = normed.reshape(tokens, n, depth).transpose(1, 0, 2)]
    pallas_call x1, Pallas kernels: 99.5 us -> 106 us  [exchange(): pl.pallas_call(functools.partial(exchange_kernel, n), out_shape=(padded,...]
  transfers between devices with their start and end apart: 1 -> 0, of which waited for: 1 -> 0; matrix products, arithmetic and copies ran while one was open for 6% -> 0% of each run, Pallas kernels for 0% -> 0%
where the time goes in v3:
time: 237 us; the launch traced here: 236 us
  Pallas kernels  191 us (81%)
  local copies, waits for them, and re-layouts  19.2 us (8%)
  matrix products  13.8 us (6%)
  other arithmetic  11.9 us (5%)
    pallas_call x1, Pallas kernels, exchange(): pl.pallas_call(functools.partial(exchange_kernel, n), out_shape=(padded,...  106 us
    pallas_call x1, Pallas kernels, gather_project(): pl.pallas_call(functools.partial(gather_kernel, n), out_shape=(jax.ShapeD...  84.8 us
    dot_general x1, matrix products, shards(): lax.dot_general(restored, whole_weight, (((1,), (1,)), ((), ())), preferr...  10.2 us
    another operation x2, local copies, waits for them, and re-layouts, gather_project(): parted = normed.reshape(tokens, n, depth).transpose(1, 0, 2)  9.58 us
    unnamed x15, local copies, waits for them, and re-layouts  5.49 us

profile of v3, /device:TPU:21, one launch (start us, length us, event | category | flops | bytes accessed | tf_op | source)
XLA Modules:
  0.0 236.3 jit_solution(13768567262072478533)
XLA Ops:
  0.6 0.0 copy-start
  0.6 0.0 copy-start.5
  0.7 0.8 dynamic_slice.3
  1.4 0.8 fusion.11.length_ref
  2.3 0.8 mul.130
  3.0 0.8 select_reduce_fusion.inverse_ref
  3.8 2.2 fusion
  6.0 0.1 multiply_sine_fusion
  6.2 1.0 fusion.10
  7.2 2.0 copy.28
  9.2 0.3 copy.29
  9.4 0.1 pad.8.upstream_ref
  9.6 0.0 copy-done
  9.6 0.4 multiply_reduce_fusion
  10.0 0.0 copy-done.5
  10.0 0.1 multiply_convert_fusion
  10.1 0.1 reshape.111
  10.2 0.0 copy-start.4
  10.3 3.2 %fusion.7 = bf16[200,2048]{1,0:T(8,128)(2,1)S(1)} fusion(bf16[200,1024]{1,0:T(8,128)(2,1)S(1)} %reshape.111, bf16[1024,2048]{1,0:T(8,128)(2,1)} %param.22), kind=kOutput, calls=%fused_computation.14 | convolution fusion | flops 839680000 | bytes 5423104 | tf_op jit(solution)/shard_map/dot_general | solution.py:45
  13.5 0.2 reshape.112
  13.7 0.1 pad.7.query_ref
  13.8 0.0 copy-done.4
  13.8 3.7 %fusion.2 = bf16[2,128,4608]{2,1,0:T(8,128)(2,1)} fusion(bf16[2,128,4608]{2,1,0:T(8,128)(2,1)} %param.12, f32[4608]{0:T(1024)S(1)} %copy-done.4, f32[2,128]{1,0:T(2,128)S(1)} %get-tuple-element.25), kind=kLoop, calls=%fused_computation.7 | loop fusion | flops 4718592 | bytes 4738048 | tf_op jit(solution)/shard_map/convert_element_type | solution.py:577
  17.5 0.0 copy-start.1
  17.5 6.9 %reshape.119 = bf16[256,16,288]{2,1,0:T(8,128)(2,1)} reshape(bf16[2,128,4608]{2,1,0:T(8,128)(2,1)} %fusion.2) | data formatting | bytes 4718592 | tf_op jit(solution)/shard_map/reshape;reshape | solution.py:512
  24.4 0.0 copy-start.2
  24.4 2.7 %copy.37 = bf16[256,16,288]{2,0,1:T(8,128)(2,1)S(1)} copy(bf16[256,16,288]{2,1,0:T(8,128)(2,1)} %reshape.119) | data formatting | bytes 4718592 | tf_op jit(solution)/shard_map/reshape;reshape | solution.py:512
  27.1 0.0 copy-done.1
  27.1 84.8 %gather_project.1 = (bf16[16,288,2048]{2,1,0:T(8,128)(2,1)}, bf16[256,2048]{1,0:T(8,128)(2,1)S(1)}) custom-call(bf16[288,2048]{1,0:T(8,128)(2,1)S(1)} %copy-done.1, bf16[16,256,288]{2,1,0:T(8,128)(2,1)S(1)} %bitcast.30), custom_call_target="tpu_custom_call" | custom-call | tf_op jit(solution)/shard_map/gather_project/pallas_call | solution.py:515
  111.9 0.0 copy-done.2
  111.9 105.8 %exchange.1 = (bf16[2,128,2048]{2,1,0:T(8,128)(2,1)S(1)}, bf16[2,128,2048]{2,1,0:T(8,128)(2,1)S(1)}, bf16[2,128,2048]{2,1,0:T(8,128)(2,1)S(1)}) custom-call(s32[32]{0:T(128)S(1)} %copy-done.2, s32[32]{0:T(128)S(1)} %select_reduce_fusion.inverse_ref, s32[2]{0:T(128)S(1)} %fusion.11.length_ref, bf16[2,128,2048]{2,1,0:T(8,128)(2,1)S(1)} %bitcast.31, ...), custom_call_target="tpu_custom_call" | custom-call | tf_op jit(solution)/shard_map/exchange/pallas_call | solution.py:310
  217.7 0.1 slice.6
  217.8 0.8 copy.30
  218.7 1.7 copy.32
  220.4 0.0 copy-start.3
  220.4 10.2 %fusion.6 = (f32[2,128]{1,0:T(2,128)S(1)}, f32[2,128,4608]{2,1,0:T(8,128)S(1)}) fusion(bf16[2,128,4608]{2,1,0:T(8,128)(2,1)} %param.12, f32[4608]{0:T(1024)S(1)} %copy-done.4, bf16[2,128,2048]{2,1,0:T(8,128)(2,1)S(1)} %get-tuple-element.10, bf16[4608,2048,1]{1,0,2:T(8,128)(2,1)} %bitcast.35), kind=kOutput, calls=%fused_computation.11 | convolution fusion | flops 4836556800 | bytes 27020288 | tf_op jit(solution)/shard_map/dot_general | solution.py:610
  230.6 0.0 copy-done.3
  230.6 3.1 %fusion.5 = bf16[2,128,4608]{2,1,0:T(8,128)(2,1)} fusion(bf16[2,128,4608]{2,1,0:T(8,128)(2,1)S(1)} %copy-done.3, f32[2,128,4608]{2,1,0:T(8,128)S(1)} %get-tuple-element.31, f32[2,128]{1,0:T(2,128)S(1)} %broadcast_multiply_fusion, f32[2,128]{1,0:T(2,128)S(1)} %get-tuple-element.24, f32[2,128]{1,0:T(2,128)S(1)} %get-tuple-element.25), kind=kLoop, calls=%fused_computation.10 | loop fusion | flops 7077888 | bytes 9440256 | tf_op jit(solution)/shard_map/convert_element_type | solution.py:617
  233.7 0.1 slice.7
  233.7 0.8 copy.31
  234.6 1.7 copy.33
  (6 shorter events, 0.0 us)
Async XLA Ops:
  0.6 8.9 %copy-start = (bf16[32,1024]{1,0:T(8,128)(2,1)S(1)}, bf16[32,1024]{1,0:T(8,128)(2,1)}, u32[]{:S(2)}) copy-start(bf16[32,1024]{1,0:T(8,128)(2,1)} %param.21) | copy-start | bytes 196612
  0.6 9.3 %copy-start.5 = (f32[1024]{0:T(1024)S(1)}, f32[1024]{0:T(1024)}, u32[]{:S(2)}) copy-start(f32[1024]{0:T(1024)} %param.20) | copy-start | bytes 12292
  10.2 3.5 %copy-start.4 = (f32[4608]{0:T(1024)S(1)}, f32[4608]{0:T(1024)}, u32[]{:S(2)}) copy-start(f32[4608]{0:T(1024)} %param.13) | copy-start | bytes 55300
  17.5 9.6 %copy-start.1 = (bf16[288,2048]{1,0:T(8,128)(2,1)S(1)}, bf16[288,2048]{1,0:T(8,128)(2,1)}, u32[]{:S(2)}) copy-start(bf16[288,2048]{1,0:T(8,128)(2,1)} %weight_ref.1) | copy-start | bytes 3538948
  24.4 87.5 %copy-start.2 = (s32[32]{0:T(128)S(1)}, s32[32]{0:T(128)}, u32[]{:S(2)}) copy-start(s32[32]{0:T(128)} %order_ref.1) | copy-start | bytes 388
  220.4 10.2 %copy-start.3 = (bf16[2,128,4608]{2,1,0:T(8,128)(2,1)S(1)}, bf16[2,128,4608]{2,1,0:T(8,128)(2,1)}, u32[]{:S(2)}) copy-start(bf16[2,128,4608]{2,1,0:T(8,128)(2,1)} %param.12) | copy-start | bytes 7077892

commit v4 on v3

--- a/solution.py
+++ b/solution.py
@@ -20,9 +20,7 @@
     return jnp.concatenate([jnp.sin(angles), jnp.cos(angles)], axis=-1)
 
 
-def expert_queries(
-    actions, flow_noise, times_in, expert_gain, action_weight, query_weight, head_dim
-):
+def expert_rows(actions, flow_noise, times_in, expert_gain, action_weight):
     batch_count, samples, horizon, action_dim = actions.shape
     model_width = action_weight.shape[1]
     flat_times = times_in.reshape(batch_count * samples)
@@ -40,11 +38,16 @@
         + time_features(flat_times, model_width)[:, None, :]
     )
     inverse_rms = lax.rsqrt(jnp.mean(hidden * hidden, axis=-1, keepdims=True) + 1e-06)
-    normed = (hidden * inverse_rms * expert_gain).astype(jnp.bfloat16).reshape(-1, model_width)
+    normed = (hidden * inverse_rms * expert_gain).astype(jnp.bfloat16)
+    return normed.reshape(batch_count, samples * horizon, model_width)
+
+
+def project_queries(normed, query_weight, head_dim):
+    flat = normed.reshape(-1, normed.shape[-1])
     queries = (
-        jnp.dot(normed, query_weight, preferred_element_type=jnp.float32) * head_dim ** (-0.5)
+        jnp.dot(flat, query_weight, preferred_element_type=jnp.float32) * head_dim ** (-0.5)
     ).astype(jnp.bfloat16)
-    return queries.reshape(batch_count, samples * horizon, query_weight.shape[1])
+    return queries.reshape(normed.shape[0], normed.shape[1], query_weight.shape[1])
 
 
 def attend(queries, keyval, length, upstream, kv_heads):
@@ -333,9 +336,13 @@
 def gather_kernel(
     n,
     weight_ref,
-    normed_ref,
+    tokens_ref,
+    expert_ref,
+    query_weight_ref,
     whole_ref,
     keyval_ref,
+    queries_ref,
+    normed_ref,
     held,
     total,
     ring_send,
@@ -426,6 +433,9 @@
     for kind in (0, 1):
         for d in (0, 1):
             ring(d, kind, 0, chip).start()
+    depth = normed_ref.shape[2]
+    for shard in range(n):
+        normed_ref[shard] = tokens_ref[:, shard * depth : (shard + 1) * depth]
     start(1, other, 1 - core).wait_recv()
 
     def product(of, which):
@@ -448,6 +458,16 @@
         return carry
 
     lax.fori_loop(0, 4, own, 0)
+
+    def query(which, carry):
+        cols = span(which * quarter, quarter)
+        product_in = jnp.dot(
+            expert_ref[...], query_weight_ref[:, cols], preferred_element_type=jnp.float32
+        )
+        queries_ref[:, cols] = (product_in * HEAD ** (-0.5)).astype(queries_ref.dtype)
+        return carry
+
+    lax.fori_loop(0, query_weight_ref.shape[1] // quarter, query, 0)
 
     def step(s, carry):
         @pl.when(s <= chips - 2)
@@ -504,29 +524,35 @@
         write(chip, which, chips - 1).wait()
 
 
-def gather_project(kv_weight, normed):
+def gather_project(kv_weight, normed, expert_normed, query_weight):
     n = lax.axis_size("seq")
     chips = n // 2
     depth, doubled = kv_weight.shape
     tokens = normed.shape[0]
-    parted = normed.reshape(tokens, n, depth).transpose(1, 0, 2)
     steps = chips - 1
     sems = pltpu.SemaphoreType.DMA
-    whole, keyval = pl.pallas_call(
+    whole, keyval, queries = pl.pallas_call(
         functools.partial(gather_kernel, n),
         out_shape=(
             jax.ShapeDtypeStruct((n, depth, doubled), jnp.bfloat16),
             jax.ShapeDtypeStruct((tokens, doubled), jnp.bfloat16),
+            jax.ShapeDtypeStruct(
+                (expert_normed.shape[0], query_weight.shape[1]), jnp.bfloat16
+            ),
         ),
         in_specs=[
             pl.BlockSpec(memory_space=pl.ANY),
+            pl.BlockSpec(memory_space=pltpu.VMEM),
+            pl.BlockSpec(memory_space=pltpu.VMEM),
             pl.BlockSpec(memory_space=pltpu.VMEM),
         ],
         out_specs=(
             pl.BlockSpec(memory_space=pl.ANY),
             pl.BlockSpec(memory_space=pltpu.VMEM),
+            pl.BlockSpec(memory_space=pltpu.VMEM),
         ),
         scratch_shapes=[
+            pltpu.VMEM((n, tokens, depth), jnp.bfloat16),
             pltpu.VMEM((n, depth, doubled), jnp.bfloat16),
             pltpu.VMEM((tokens, doubled), jnp.float32),
             sems((2, 2, steps)),
@@ -540,11 +566,11 @@
             sems((2, 2, chips + 1)),
         ],
         compiler_params=pltpu.CompilerParams(
-            collective_id=1, has_side_effects=True, vmem_limit_bytes=48 * 2**20
+            collective_id=1, has_side_effects=True, vmem_limit_bytes=54 * 2**20
         ),
         name="gather_project",
-    )(kv_weight, parted)
-    return whole.reshape(n * depth, doubled), keyval
+    )(kv_weight, normed, expert_normed, query_weight)
+    return whole.reshape(n * depth, doubled), keyval, queries
 
 
 def shards(
@@ -579,15 +605,19 @@
     )
     n = lax.axis_size("seq")
     fits = doubled // n == HEAD and kv_weight.shape[0] % 16 == 0
-    if fits and n % 4 == 0 and lax.axis_size("parts") == 2:
-        whole_weight, product = gather_project(kv_weight, normed)
+    fits = fits and n % 4 == 0 and lax.axis_size("parts") == 2
+    row_count = samples * horizon
+    extra = ((0, 0), (0, positions - row_count), (0, 0))
+    expert = expert_rows(actions, flow_noise, timesteps, expert_gain, action_weight)
+    if fits:
+        flat = jnp.pad(expert, extra).reshape(owned_count * positions, expert.shape[-1])
+        whole_weight, product, queries = gather_project(kv_weight, normed, flat, query_weight)
+        queries = queries.reshape(owned_count, positions, q_width)
     else:
         whole_weight = lax.all_gather(kv_weight, "seq", axis=0, tiled=True)
         product = jnp.dot(normed, whole_weight, preferred_element_type=jnp.float32)
+        queries = project_queries(expert, query_weight, HEAD)
     keyval = product.astype(jnp.bfloat16).reshape(owned_count, positions, doubled)
-    queries = expert_queries(
-        actions, flow_noise, timesteps, expert_gain, action_weight, query_weight, HEAD
-    )
     upstream = grad_attended.reshape(owned_count, samples * horizon, q_width)
     slot_index = jnp.arange(episodes, dtype=jnp.int32)
     matches = assign[None, :] == slot_index[:, None]
@@ -595,11 +625,9 @@
     my_slots = lax.dynamic_slice_in_dim(assign, position * owned_count, owned_count)
     chosen = slot_index[None, :] == my_slots[:, None]
     owned_len = jnp.sum(jnp.where(chosen, lengths[None, :], 0), axis=1)
-    if doubled // n == HEAD:
-        row_count = samples * horizon
-        extra = ((0, 0), (0, positions - row_count), (0, 0))
+    if fits:
         attended, grad_query, grad_keyval = exchange(
-            assign, inverse, owned_len, keyval, jnp.pad(queries, extra), jnp.pad(upstream, extra)
+            assign, inverse, owned_len, keyval, queries, jnp.pad(upstream, extra)
         )
         attended, grad_query = attended[:, :row_count], grad_query[:, :row_count]
     else:

time: 237 us -> 226 us (0.954)
  local copies, waits for them, and re-layouts: 19.2 us -> 8.56 us
  Pallas kernels: 191 us -> 195 us
  matrix products: 13.8 us -> 9.92 us
    another operation x2 -> x0, local copies, waits for them, and re-layouts: 9.58 us -> none  [gather_project(): parted = normed.reshape(tokens, n, depth).transpose(1, 0, 2)]
    pallas_call x1, Pallas kernels: 84.8 us -> 90.1 us  [gather_project(): pl.pallas_call(functools.partial(gather_kernel, n), out_shape=(jax.ShapeD...]
    dot_general x2 -> x1, matrix products: 3.6 us -> 0.39 us  [expert_rows(): jnp.dot(noisy_actions.reshape(-1, action_dim).astype(jnp.bfloat16), actio...]
    unnamed x15 -> x25, local copies, waits for them, and re-layouts: 5.49 us -> 4.61 us
where the time goes in v4:
time: 226 us
  Pallas kernels  195 us (86%)
  other arithmetic  11.1 us (5%)
  matrix products  9.92 us (4%)
  local copies, waits for them, and re-layouts  8.56 us (4%)
    pallas_call x1, Pallas kernels, exchange(): pl.pallas_call(functools.partial(exchange_kernel, n), out_shape=(padded,...  105 us
    pallas_call x1, Pallas kernels, gather_project(): pl.pallas_call(functools.partial(gather_kernel, n), out_shape=(jax.ShapeD...  90.1 us
    dot_general x1, matrix products, shards(): lax.dot_general(restored, whole_weight, (((1,), (1,)), ((), ())), preferr...  9.53 us
    unnamed x25, local copies, waits for them, and re-layouts  4.61 us

profile of v4, /device:TPU:21, one launch (start us, length us, event | category | flops | bytes accessed | tf_op | source)
XLA Modules:
  0.0 225.8 jit_solution(15744601226396885736)
XLA Ops:
  0.6 0.0 copy-start
  0.6 0.0 copy-start.10
  0.7 0.0 copy-start.6
  0.7 0.0 copy-start.7
  0.7 0.0 copy-start.9
  0.7 0.8 select_reduce_fusion.inverse_ref
  1.5 0.7 dynamic_slice.3
  2.3 0.8 fusion.10.length_ref
  3.1 2.2 fusion
  5.3 3.7 %fusion.2 = bf16[2,128,4608]{2,1,0:T(8,128)(2,1)} fusion(bf16[2,128,4608]{2,1,0:T(8,128)(2,1)} %param.12, f32[4608]{0:T(1024)} %param.13, f32[2,128]{1,0:T(2,128)S(1)} %get-tuple-element.27), kind=kLoop, calls=%fused_computation.7 | loop fusion | flops 4718592 | bytes 4738048 | tf_op jit(solution)/shard_map/convert_element_type | solution.py:603
  9.0 0.0 copy-done.10
  9.0 0.1 mul.124
  9.1 0.1 multiply_sine_fusion
  9.3 0.0 copy-done.6
  9.3 0.0 copy-done.7
  9.3 0.1 fusion.9
  9.4 0.0 copy-done
  9.4 0.4 multiply_reduce_fusion
  9.8 0.0 copy-done.9
  9.8 0.1 multiply_convert_fusion
  10.0 0.1 reshape.117
  10.1 0.0 copy-start.5
  10.1 0.9 pad.8
  10.9 0.0 copy-start.3
  10.9 90.1 %gather_project.1 = (bf16[16,288,2048]{2,1,0:T(8,128)(2,1)}, bf16[256,2048]{1,0:T(8,128)(2,1)}, bf16[256,2048]{1,0:T(8,128)(2,1)}) custom-call(bf16[288,2048]{1,0:T(8,128)(2,1)} %weight_ref.1, bf16[256,4608]{1,0:T(8,128)(2,1)} %bitcast.30, bf16[256,1024]{1,0:T(8,128)(2,1)} %bitcast.34, bf16[1024,2048]{1,0:T(8,128)(2,1)} %query_weight_ref.1), custom_call_target="tpu_custom_call" | custom-call | tf_op jit(solution)/shard_map/gather_project/pallas_call | solution.py:534
  101.1 0.0 copy-start.1
  101.1 0.0 copy-start.2
  101.1 0.0 copy-done.5
  101.1 0.8 copy.24
  102.0 0.3 copy.25
  102.2 0.0 copy-start.4
  102.3 0.0 copy-start.8
  102.3 0.1 pad.9.upstream_ref
  102.4 0.0 copy-done.3
  102.4 0.0 copy-done.1
  102.4 0.2 copy-done.2
  102.6 105.2 %exchange.1 = (bf16[2,128,2048]{2,1,0:T(8,128)(2,1)S(1)}, bf16[2,128,2048]{2,1,0:T(8,128)(2,1)S(1)}, bf16[2,128,2048]{2,1,0:T(8,128)(2,1)S(1)}) custom-call(s32[32]{0:T(128)S(1)} %copy-done.3, s32[32]{0:T(128)S(1)} %select_reduce_fusion.inverse_ref, s32[2]{0:T(128)S(1)} %fusion.10.length_ref, bf16[2,128,2048]{2,1,0:T(8,128)(2,1)S(1)} %bitcast.28, ...), custom_call_target="tpu_custom_call" | custom-call | tf_op jit(solution)/shard_map/exchange/pallas_call | solution.py:313
  207.9 0.1 slice.6
  208.0 0.8 copy.26
  208.8 1.7 copy.28
  210.5 0.0 copy-done.4
  210.5 0.0 copy-done.8
  210.6 9.5 %fusion.6 = (f32[2,128]{1,0:T(2,128)S(1)}, f32[2,128,4608]{2,1,0:T(8,128)S(1)}) fusion(bf16[2,128,4608]{2,1,0:T(8,128)(2,1)S(1)} %copy-done.4, f32[4608]{0:T(1024)S(1)} %copy-done.8, bf16[2,128,2048]{2,1,0:T(8,128)(2,1)S(1)} %get-tuple-element.12, bf16[4608,2048,1]{1,0,2:T(8,128)(2,1)} %bitcast.35), kind=kOutput, calls=%fused_computation.11 | convolution fusion | flops 4836556800 | bytes 27020288 | tf_op jit(solution)/shard_map/dot_general | solution.py:638
  220.1 3.1 %fusion.5 = bf16[2,128,4608]{2,1,0:T(8,128)(2,1)} fusion(bf16[2,128,4608]{2,1,0:T(8,128)(2,1)S(1)} %copy-done.4, f32[2,128,4608]{2,1,0:T(8,128)S(1)} %get-tuple-element.33, f32[2,128]{1,0:T(2,128)S(1)} %broadcast_multiply_fusion, f32[2,128]{1,0:T(2,128)S(1)} %get-tuple-element.26, f32[2,128]{1,0:T(2,128)S(1)} %get-tuple-element.27), kind=kLoop, calls=%fused_computation.10 | loop fusion | flops 7077888 | bytes 9440256 | tf_op jit(solution)/shard_map/convert_element_type | solution.py:645
  223.2 0.1 slice.7
  223.3 0.8 copy.27
  224.1 1.7 copy.29
  (6 shorter events, 0.0 us)
Async XLA Ops:
  0.6 8.8 %copy-start = (bf16[32,1024]{1,0:T(8,128)(2,1)S(1)}, bf16[32,1024]{1,0:T(8,128)(2,1)}, u32[]{:S(2)}) copy-start(bf16[32,1024]{1,0:T(8,128)(2,1)} %param.21) | copy-start | bytes 196612
  0.6 8.4 %copy-start.10 = (f32[2,2]{1,0:T(2,128)S(1)}, f32[2,2]{1,0:T(2,128)}, u32[]{:S(2)}) copy-start(f32[2,2]{1,0:T(2,128)} %param.19) | copy-start | bytes 52
  0.7 8.6 %copy-start.6 = (f32[2,2,50,32]{2,3,1,0:T(8,128)S(1)}, f32[2,2,50,32]{2,3,1,0:T(8,128)}, u32[]{:S(2)}) copy-start(f32[2,2,50,32]{2,3,1,0:T(8,128)} %param.17) | copy-start | bytes 76804
  0.7 8.6 %copy-start.7 = (f32[2,2,50,32]{2,3,1,0:T(8,128)S(1)}, f32[2,2,50,32]{2,3,1,0:T(8,128)}, u32[]{:S(2)}) copy-start(f32[2,2,50,32]{2,3,1,0:T(8,128)} %param.18) | copy-start | bytes 76804
  0.7 9.1 %copy-start.9 = (f32[1024]{0:T(1024)S(1)}, f32[1024]{0:T(1024)}, u32[]{:S(2)}) copy-start(f32[1024]{0:T(1024)} %param.20) | copy-start | bytes 12292
  10.1 91.0 %copy-start.5 = (bf16[2,2,50,2048]{3,1,2,0:T(2,128)(2,1)S(1)}, bf16[2,2,50,2048]{3,1,2,0:T(2,128)(2,1)}, u32[]{:S(2)}) copy-start(bf16[2,2,50,2048]{3,1,2,0:T(2,128)(2,1)} %param.23) | copy-start | bytes 2457604
  10.9 91.4 %copy-start.3 = (s32[32]{0:T(128)S(1)}, s32[32]{0:T(128)}, u32[]{:S(2)}) copy-start(s32[32]{0:T(128)} %order_ref.1) | copy-start | bytes 388
  101.1 1.3 copy-start.1
  101.1 1.5 copy-start.2
  102.2 108.3 %copy-start.4 = (bf16[2,128,4608]{2,1,0:T(8,128)(2,1)S(1)}, bf16[2,128,4608]{2,1,0:T(8,128)(2,1)}, u32[]{:S(2)}) copy-start(bf16[2,128,4608]{2,1,0:T(8,128)(2,1)} %param.12) | copy-start | bytes 7077892
  102.3 108.3 %copy-start.8 = (f32[4608]{0:T(1024)S(1)}, f32[4608]{0:T(1024)}, u32[]{:S(2)}) copy-start(f32[4608]{0:T(1024)} %param.13) | copy-start | bytes 55300

commit v5 on v4

--- a/solution.py
+++ b/solution.py
@@ -139,7 +139,6 @@
     me = lax.axis_index("seq")
     own = keyval_ref.shape[0]
     heads = KV_HEADS
-    episodes = spread.shape[0]
 
     def columns(index):
         return pl.ds(pl.multiple_of(index * HEAD, HEAD), HEAD)
@@ -186,14 +185,9 @@
     kept.wait()
     others(lambda d: first_in(d).wait_recv())
 
-    def arrange(source, target, order):
-        def step(e, carry):
-            target[e] = source[order[e]]
-            return carry
-
-        lax.fori_loop(0, episodes, step, 0)
-
-    arrange(spread, arranged, order_ref)
+    def arrange(source, target, order, d):
+        for e in range(own):
+            target[d * own + e] = source[order[d * own + e]]
 
     def second(d):
         return remote(1, arranged.at[rows(d)], owned.at[:, :, columns(me)], d, me)
@@ -201,11 +195,17 @@
     def second_in(d):
         return remote(1, arranged.at[rows(d)], owned.at[:, :, columns(d)], d, d)
 
+    arrange(spread, arranged, order_ref, me)
     kept = pltpu.make_async_copy(
         arranged.at[rows(me)], owned.at[:, :, columns(me)], local_sems.at[1]
     )
     kept.start()
-    others(lambda d: second(d).start())
+
+    def second_out(d):
+        arrange(spread, arranged, order_ref, d)
+        second(d).start()
+
+    others(second_out)
     kept.wait()
 
     def third(d):
@@ -276,7 +276,6 @@
     kept.start()
     kept.wait()
     others(lambda d: third_in(d).wait_recv())
-    arrange(spread_back, arranged_back, inverse_ref)
 
     def fourth(d):
         return remote(3, arranged_back.at[rows(d)], restored_ref.at[:, :, columns(me)], d, me)
@@ -284,11 +283,17 @@
     def fourth_in(d):
         return remote(3, arranged_back.at[rows(d)], restored_ref.at[:, :, columns(d)], d, d)
 
+    arrange(spread_back, arranged_back, inverse_ref, me)
     kept = pltpu.make_async_copy(
         arranged_back.at[rows(me)], restored_ref.at[:, :, columns(me)], local_sems.at[3]
     )
     kept.start()
-    others(lambda d: fourth(d).start())
+
+    def fourth_out(d):
+        arrange(spread_back, arranged_back, inverse_ref, d)
+        fourth(d).start()
+
+    others(fourth_out)
     kept.wait()
     others(lambda d: fourth_in(d).wait_recv())
 

time: 226 us -> 226 us (level)
  no operation moved by 1% of the time
where the time goes in v5:
time: 226 us
  Pallas kernels  195 us (86%)
  other arithmetic  11.1 us (5%)
  matrix products  9.91 us (4%)
  local copies, waits for them, and re-layouts  8.56 us (4%)
    pallas_call x1, Pallas kernels, exchange(): pl.pallas_call(functools.partial(exchange_kernel, n), out_shape=(padded,...  105 us
    pallas_call x1, Pallas kernels, gather_project(): pl.pallas_call(functools.partial(gather_kernel, n), out_shape=(jax.ShapeD...  90.1 us
    dot_general x1, matrix products, shards(): lax.dot_general(restored, whole_weight, (((1,), (1,)), ((), ())), preferr...  9.53 us
    unnamed x25, local copies, waits for them, and re-layouts  4.61 us

profile of v5, /device:TPU:21, one launch (start us, length us, event | category | flops | bytes accessed | tf_op | source)
XLA Modules:
  0.0 225.6 jit_solution(1789468993477991345)
XLA Ops:
  0.6 0.0 copy-start
  0.6 0.0 copy-start.10
  0.7 0.0 copy-start.6
  0.7 0.0 copy-start.7
  0.7 0.0 copy-start.9
  0.7 0.8 select_reduce_fusion.inverse_ref
  1.5 0.7 dynamic_slice.3
  2.3 0.8 fusion.10.length_ref
  3.1 2.2 fusion
  5.3 3.7 %fusion.2 = bf16[2,128,4608]{2,1,0:T(8,128)(2,1)} fusion(bf16[2,128,4608]{2,1,0:T(8,128)(2,1)} %param.12, f32[4608]{0:T(1024)} %param.13, f32[2,128]{1,0:T(2,128)S(1)} %get-tuple-element.27), kind=kLoop, calls=%fused_computation.7 | loop fusion | flops 4718592 | bytes 4738048 | tf_op jit(solution)/shard_map/convert_element_type | solution.py:608
  9.0 0.0 copy-done.10
  9.0 0.1 mul.124
  9.1 0.1 multiply_sine_fusion
  9.3 0.0 copy-done.6
  9.3 0.0 copy-done.7
  9.3 0.1 fusion.9
  9.4 0.0 copy-done
  9.4 0.4 multiply_reduce_fusion
  9.8 0.0 copy-done.9
  9.8 0.1 multiply_convert_fusion
  10.0 0.1 reshape.117
  10.1 0.0 copy-start.5
  10.1 0.9 pad.8
  10.9 0.0 copy-start.3
  10.9 90.1 %gather_project.1 = (bf16[16,288,2048]{2,1,0:T(8,128)(2,1)}, bf16[256,2048]{1,0:T(8,128)(2,1)}, bf16[256,2048]{1,0:T(8,128)(2,1)}) custom-call(bf16[288,2048]{1,0:T(8,128)(2,1)} %weight_ref.1, bf16[256,4608]{1,0:T(8,128)(2,1)} %bitcast.30, bf16[256,1024]{1,0:T(8,128)(2,1)} %bitcast.34, bf16[1024,2048]{1,0:T(8,128)(2,1)} %query_weight_ref.1), custom_call_target="tpu_custom_call" | custom-call | tf_op jit(solution)/shard_map/gather_project/pallas_call | solution.py:539
  101.1 0.0 copy-start.1
  101.1 0.0 copy-start.2
  101.1 0.0 copy-done.5
  101.1 0.8 copy.24
  102.0 0.3 copy.25
  102.2 0.0 copy-start.4
  102.3 0.0 copy-start.8
  102.3 0.1 pad.9.upstream_ref
  102.4 0.0 copy-done.3
  102.4 0.0 copy-done.1
  102.4 0.2 copy-done.2
  102.6 105.0 %exchange.1 = (bf16[2,128,2048]{2,1,0:T(8,128)(2,1)S(1)}, bf16[2,128,2048]{2,1,0:T(8,128)(2,1)S(1)}, bf16[2,128,2048]{2,1,0:T(8,128)(2,1)S(1)}) custom-call(s32[32]{0:T(128)S(1)} %copy-done.3, s32[32]{0:T(128)S(1)} %select_reduce_fusion.inverse_ref, s32[2]{0:T(128)S(1)} %fusion.10.length_ref, bf16[2,128,2048]{2,1,0:T(8,128)(2,1)S(1)} %bitcast.28, ...), custom_call_target="tpu_custom_call" | custom-call | tf_op jit(solution)/shard_map/exchange/pallas_call | solution.py:318
  207.7 0.1 slice.6
  207.7 0.8 copy.26
  208.6 1.7 copy.28
  210.3 0.0 copy-done.4
  210.3 0.0 copy-done.8
  210.3 9.5 %fusion.6 = (f32[2,128]{1,0:T(2,128)S(1)}, f32[2,128,4608]{2,1,0:T(8,128)S(1)}) fusion(bf16[2,128,4608]{2,1,0:T(8,128)(2,1)S(1)} %copy-done.4, f32[4608]{0:T(1024)S(1)} %copy-done.8, bf16[2,128,2048]{2,1,0:T(8,128)(2,1)S(1)} %get-tuple-element.12, bf16[4608,2048,1]{1,0,2:T(8,128)(2,1)} %bitcast.35), kind=kOutput, calls=%fused_computation.11 | convolution fusion | flops 4836556800 | bytes 27020288 | tf_op jit(solution)/shard_map/dot_general | solution.py:643
  219.9 3.1 %fusion.5 = bf16[2,128,4608]{2,1,0:T(8,128)(2,1)} fusion(bf16[2,128,4608]{2,1,0:T(8,128)(2,1)S(1)} %copy-done.4, f32[2,128,4608]{2,1,0:T(8,128)S(1)} %get-tuple-element.33, f32[2,128]{1,0:T(2,128)S(1)} %broadcast_multiply_fusion, f32[2,128]{1,0:T(2,128)S(1)} %get-tuple-element.26, f32[2,128]{1,0:T(2,128)S(1)} %get-tuple-element.27), kind=kLoop, calls=%fused_computation.10 | loop fusion | flops 7077888 | bytes 9440256 | tf_op jit(solution)/shard_map/convert_element_type | solution.py:650
  222.9 0.1 slice.7
  223.0 0.8 copy.27
  223.9 1.7 copy.29
  (6 shorter events, 0.0 us)
Async XLA Ops:
  0.6 8.8 %copy-start = (bf16[32,1024]{1,0:T(8,128)(2,1)S(1)}, bf16[32,1024]{1,0:T(8,128)(2,1)}, u32[]{:S(2)}) copy-start(bf16[32,1024]{1,0:T(8,128)(2,1)} %param.21) | copy-start | bytes 196612
  0.6 8.4 %copy-start.10 = (f32[2,2]{1,0:T(2,128)S(1)}, f32[2,2]{1,0:T(2,128)}, u32[]{:S(2)}) copy-start(f32[2,2]{1,0:T(2,128)} %param.19) | copy-start | bytes 52
  0.7 8.6 %copy-start.6 = (f32[2,2,50,32]{2,3,1,0:T(8,128)S(1)}, f32[2,2,50,32]{2,3,1,0:T(8,128)}, u32[]{:S(2)}) copy-start(f32[2,2,50,32]{2,3,1,0:T(8,128)} %param.17) | copy-start | bytes 76804
  0.7 8.6 %copy-start.7 = (f32[2,2,50,32]{2,3,1,0:T(8,128)S(1)}, f32[2,2,50,32]{2,3,1,0:T(8,128)}, u32[]{:S(2)}) copy-start(f32[2,2,50,32]{2,3,1,0:T(8,128)} %param.18) | copy-start | bytes 76804
  0.7 9.1 %copy-start.9 = (f32[1024]{0:T(1024)S(1)}, f32[1024]{0:T(1024)}, u32[]{:S(2)}) copy-start(f32[1024]{0:T(1024)} %param.20) | copy-start | bytes 12292
  10.1 91.0 %copy-start.5 = (bf16[2,2,50,2048]{3,1,2,0:T(2,128)(2,1)S(1)}, bf16[2,2,50,2048]{3,1,2,0:T(2,128)(2,1)}, u32[]{:S(2)}) copy-start(bf16[2,2,50,2048]{3,1,2,0:T(2,128)(2,1)} %param.23) | copy-start | bytes 2457604
  10.9 91.4 %copy-start.3 = (s32[32]{0:T(128)S(1)}, s32[32]{0:T(128)}, u32[]{:S(2)}) copy-start(s32[32]{0:T(128)} %order_ref.1) | copy-start | bytes 388
  101.1 1.3 copy-start.1
  101.1 1.5 copy-start.2
  102.2 108.1 %copy-start.4 = (bf16[2,128,4608]{2,1,0:T(8,128)(2,1)S(1)}, bf16[2,128,4608]{2,1,0:T(8,128)(2,1)}, u32[]{:S(2)}) copy-start(bf16[2,128,4608]{2,1,0:T(8,128)(2,1)} %param.12) | copy-start | bytes 7077892
  102.3 108.1 %copy-start.8 = (f32[4608]{0:T(1024)S(1)}, f32[4608]{0:T(1024)}, u32[]{:S(2)}) copy-start(f32[4608]{0:T(1024)} %param.13) | copy-start | bytes 55300
